TPU v7x, 32 devices: a whole 2x2x4 slice. The times are simulated.
32 devices in a mesh: nest: 2 (over x), tile: 16 (over z, y, core).
Axes of the slice: x: 2, y: 2, z: 4, core: 2. Of those that a mesh axis runs over, the one named last changes fastest.
Arguments:
- fine_level: float32 [2, 1280, 640], P('nest', 'tile'), may hold values from -4 to 4
- fine_flux: float32 [2, 2, 1280, 640], P('nest', None, 'tile'), may hold values from -3 to 3
- fine_depth: float32 [2, 1280, 640], P('nest', 'tile'), may hold values from 0.5 to 2
- shoreline: int32 [2, 1280], P('nest', 'tile'), may hold values from 0 to 319
- extents: int32 [2, 16], P('nest', 'tile'), may hold values from 0 to 80, as said below
- intersection: int32 [2, 2], replicated, may hold values from 0 to 383, as said below
- parent_level: float32 [256, 512], P('tile'), may hold values from -4 to 4
- parent_flux: float32 [2, 256, 512], P(None, 'tile'), may hold values from -3 to 3
- parent_depth: float32 [256, 512], P('tile'), may hold values from 0.5 to 2
- wind_stress: float32 [2, 256, 512], P(None, 'tile'), may hold values from -3 to 3
Outputs:
- fine_level_out: float32 [2, 1280, 640], P('nest', 'tile')
- fine_flux_out: float32 [2, 2, 1280, 640], P('nest', None, 'tile')
- parent_level_out: float32 [256, 512], P('tile')
- parent_flux_out: float32 [2, 256, 512], P(None, 'tile')
Inputs may be any that keep to these rules, and one draw needn't show every extreme that they name: `intersection`: row offsets are below 16; nest 0's row offset is at least 1 and nest 1's is 0. First columns are at most 383, and one nest's first column is exactly that. `extents`: within each nest, tiles are fully active up to one partly active tile, and inactive after it; nest 0 is fully active.
All inputs are finite; a program needn't handle non-finite values.
Results may differ from a plain program's by a relative error of at most 0.0003.
Values sent between devices are 32-bit elements; how exact they have to be, the bound alone decides.
A program may use at most 64 MiB of HBM per device.

v0:
```python
import functools

import jax
import jax.numpy as jnp
from jax import lax
from jax.experimental import pallas as pl
from jax.experimental.pallas import tpu as pltpu
from jax.sharding import PartitionSpec as P

RATIO = 5
SUBSTEPS = 4
DT_FINE = 0.4
DT_COARSE = 1.6
DX_COARSE = 5.0
FRICTION = 0.05
RF = 1.0 / (1.0 + DT_FINE * FRICTION)
RP = 1.0 / (1.0 + DT_COARSE * FRICTION)
CP = DT_COARSE / DX_COARSE
FAR = 1.0e6
WIN = 112
CH = 16


def parts_of(x, n):
    out = []
    for _ in range(n):
        hi = x.astype(jnp.bfloat16)
        out.append(hi)
        x = x - hi.astype(jnp.float32)
    return out


def mm(a, b):
    return lax.dot_general(a, b, (((1,), (0,)), ((), ())), preferred_element_type=jnp.float32)


def left_hot(hot, x, n):
    return sum(mm(hot, p) for p in parts_of(x, n))


def right_hot(x, hot, n):
    return sum(mm(p, hot) for p in parts_of(x, n))


def hot_of(mask):
    return jnp.where(mask, 1.0, 0.0).astype(jnp.bfloat16)


def iota(shape, axis):
    return lax.broadcasted_iota(jnp.int32, shape, axis)


def fdiv5(x):
    return jnp.floor((x.astype(jnp.float32) + 0.5) * 0.2).astype(jnp.int32)


def shift_rows(x, by):
    return pltpu.roll(x, by % x.shape[0], 0)


def shift_cols(x, by):
    return pltpu.roll(x, by % x.shape[1], 1)


def parent_step(e, ux, uy, hx, hy, wx, wy, col_open, row_open):
    nx = col_open * (ux - CP * hx * (shift_cols(e, -1) - e) + DT_COARSE * wx) * RP
    ny = row_open * (uy - CP * hy * (shift_rows(e, -1) - e) + DT_COARSE * wy) * RP
    return nx, ny


def kernel(
    T, height, breadth, ph, pc,
    fl, ff, fd, shore, ext, inter, plev_h, pflux_h, pdep_h, wind_h,
    fl_out, ff_out, pl_out, pf_out,
    e, q, dep, lim, fxr, cx, fyr, cy, sea0, sead, er, qr, pfv, wv,
    shv, exs, ins, xlev, xdep, xuy, xwy, pws, pwb, pks, pkb, ss1, fs1, ss2, fs2, p2s, p2b,
    sa, ra, sb, rb, sc, rc, sd, rd, se, re_, sl_,
):
    k = lax.axis_index("nest")
    t = lax.axis_index("tile")
    ko = 1 - k
    top = 16
    rows = height + 32

    def have(d):
        return (t + d >= 0) & (t + d < T)

    small = [
        pltpu.make_async_copy(src, dst, sl_.at[7 + i])
        for i, (src, dst) in enumerate(((shore, shv), (ext, exs), (inter, ins)))
    ]
    for c in small:
        c.start()
    barrier = pltpu.get_barrier_semaphore()
    greet = [(k, -2), (k, -1), (k, 1), (k, 2)] + [(ko, d) for d in (-2, -1, 0, 1, 2)]
    count = 1
    for nest, d in greet:
        if d == 0:
            pl.semaphore_signal(barrier, inc=1, device_id=(nest, t), device_id_type=pl.DeviceIdType.MESH)
        else:
            @pl.when(have(d))
            def _():
                pl.semaphore_signal(barrier, inc=1, device_id=(nest, t + d), device_id_type=pl.DeviceIdType.MESH)
            count = count + have(d).astype(jnp.int32)

    class Push:
        def __init__(self, src, dst, ssem, rsem, nest, d):
            self.d, self.dst = d, dst
            self.c = pltpu.make_async_remote_copy(
                src_ref=src, dst_ref=dst, send_sem=ssem, recv_sem=rsem,
                device_id=(nest, t + d), device_id_type=pl.DeviceIdType.MESH)

        def start(self):
            if self.d == 0:
                self.c.start()
            else:
                pl.when(have(self.d))(lambda: self.c.start())

        def sent(self):
            if self.d == 0:
                self.c.wait_send()
            else:
                pl.when(have(self.d))(lambda: self.c.wait_send())

        def arrive(self, fill=0.0):
            if self.d == 0:
                self.c.wait_recv()
            else:
                pl.when(have(-self.d))(lambda: self.c.wait_recv())

                @pl.when(jnp.logical_not(have(-self.d)))
                def _():
                    self.dst[...] = jnp.full(self.dst.shape, fill, jnp.float32)

    mid = slice(top, top + height)
    own = slice(8, 8 + ph)
    local = [
        pltpu.make_async_copy(src, dst, sl_.at[i])
        for i, (src, dst) in enumerate((
            (plev_h, xlev.at[own, :]), (pflux_h, pfv), (pdep_h, xdep.at[own, :]), (wind_h, wv),
            (fd.at[0], dep.at[mid, :]), (fl.at[0], e.at[mid, :]), (ff.at[0], q.at[:, mid, :]),
        ))
    ]
    for c in local:
        c.start()

    pl.semaphore_wait(barrier, count)
    round_a = []
    n = 0
    for d in (1, -1):
        hown = slice(height - 8, height) if d == 1 else slice(0, 8)
        lown = slice(top + height - 8, top + height) if d == 1 else slice(top, top + 8)
        to = slice(top - 8, top) if d == 1 else slice(top + height, top + height + 8)
        pown = slice(ph - 8, ph) if d == 1 else slice(0, 8)
        pto = slice(0, 8) if d == 1 else slice(8 + ph, 16 + ph)
        slot = 0 if d == 1 else 2
        for src, dst in (
            (pws.at[:, :, :], pwb.at[:, slot * ph:(slot + 1) * ph, :]),
            (lim.at[lown, :], lim.at[to, :]),
            (fd.at[0, hown, :], dep.at[to, :]),
            (fl.at[0, hown, :], e.at[to, :]),
            (ff.at[0, :, hown, :], q.at[:, to, :]),
            (plev_h.at[pown, :], xlev.at[pto, :]),
            (pdep_h.at[pown, :], xdep.at[pto, :]),
            (pflux_h.at[1, pown, :], xuy.at[pto, :]),
            (wind_h.at[1, pown, :], xwy.at[pto, :]),
        ):
            round_a.append(Push(src, dst, sa.at[n], ra.at[n], k, d))
            n += 1
    round_a.append(Push(pws.at[:, :, :], pwb.at[:, 3 * ph:4 * ph, :], sa.at[n], ra.at[n], k, -2))
    fine_halo = round_a[1:5] + round_a[10:14]
    windows = [round_a[0], round_a[9], round_a[18]]
    parent_halo = round_a[5:9] + round_a[14:18]
    early = round_a[2:5] + round_a[11:14]
    for c in early:
        c.start()
    for c in small:
        c.wait()
    offset = jnp.where(k == 0, ins[0, 0], ins[1, 0])
    col_a = jnp.where(k == 0, ins[0, 1], ins[1, 1])
    col_b = jnp.where(k == 0, ins[1, 1], ins[0, 1])

    diag = iota((height, height), 0) == iota((height, height), 1)
    limit = jnp.sum(jnp.where(diag, shv[...].astype(jnp.float32), 0.0), axis=1, keepdims=True)
    r = iota((height, 128), 0)
    live = (r < exs[0, 0]) & (offset + t * (height // RATIO) + fdiv5(r) < ph * T)
    lim[top:top + height, :] = jnp.where(live, limit, FAR)

    lane512 = iota((pc, 128), 0)
    take = hot_of(lane512 == col_a + WIN + (iota((pc, 128), 1) & 31))
    for c in local[:4]:
        c.wait()
    plev, pdep = xlev[own, :], xdep[own, :]
    xuy[own, :] = pfv[1]
    xwy[own, :] = wv[1]
    stack = jnp.concatenate([plev, pfv[0], pfv[1], pdep, wv[0], wv[1]], axis=0)
    win = right_hot(stack, take, 3)
    group = iota((ph, 128), 1) >> 5
    pack0 = jnp.zeros((ph, 128), jnp.float32)
    pack1 = jnp.zeros((ph, 128), jnp.float32)
    for i in range(4):
        pack0 = jnp.where(group == i, win[i * ph:(i + 1) * ph], pack0)
    for i in range(2):
        pack1 = jnp.where(group == i, win[(4 + i) * ph:(5 + i) * ph], pack1)
    pws[0] = pack0
    pws[1] = pack1

    for c in [round_a[1], round_a[10]] + windows + parent_halo:
        c.start()

    zpad = jnp.zeros((8, breadth), jnp.float32)
    for s in (slice(0, 8), slice(rows - 8, rows)):
        e[s, :] = zpad
        dep[s, :] = zpad
        q[0, s, :] = zpad
        q[1, s, :] = zpad
        lim[s, :] = jnp.full((8, 128), FAR, jnp.float32)
    pwb[:, ph:2 * ph, :] = pws[...]

    colc = iota((CH, breadth), 1)
    last = colc == breadth - 1
    reps = breadth // 128

    def coefficients(r0):
        sl = slice(r0, r0 + CH)
        ss = slice(r0 + 1, r0 + CH + 1)
        colf = colc.astype(jnp.float32)
        wide = lambda s: jnp.concatenate([lim[s, :]] * reps, axis=1)
        act = jnp.where(colf >= wide(sl), 1.0, 0.0)
        act_s = jnp.where(colf >= wide(ss), 1.0, 0.0)
        d0 = dep[sl, :]
        fx = jnp.where(last, 0.0, act * shift_cols(act, -1))
        fxr[sl, :] = fx * RF
        cx[sl, :] = jnp.where(
            last, act * jnp.sqrt(d0), (DT_FINE * RF * 0.5) * fx * (d0 + shift_cols(d0, -1)))
        fy = act * act_s
        fyr[sl, :] = fy * RF
        cy[sl, :] = (DT_FINE * RF * 0.5) * fy * (d0 + dep[ss, :])

    local[4].wait()
    for r0 in range(8 + CH, rows - 8 - CH, CH):
        coefficients(r0)
    for c in local[5:]:
        c.wait()
    for c in fine_halo:
        c.arrive(FAR if c is round_a[1] or c is round_a[10] else 0.0)
    coefficients(8)
    coefficients(rows - 8 - CH)

    def window_step(we, wux, wuy):
        nx, ny = parent_step(we, wux, wuy, whx, why, wwx, wwy, w_col_open, w_row_open)
        ne = we - CP * (nx - shift_cols(nx, 1) + ny - shift_rows(ny, 1))
        return ne, nx, ny

    lane = iota((4 * ph, 128), 1)
    lane_f = iota((rows - 16, 128), 1)
    lev_at = 128 - WIN
    flux_at = 127 - WIN

    def set_sea(oe, oux, ne, nux):
        z = jnp.where(lane == 127, shift_cols(oe, 127 - lev_at), 0.0)
        z = jnp.where(lane == 126, shift_cols(oux, 126 - flux_at), z)
        z = jnp.where(lane == 125, shift_cols(ne, 125 - lev_at), z)
        z = jnp.where(lane == 124, shift_cols(nux, 124 - flux_at), z)
        s = left_hot(spread, z, 3)
        act = jnp.where(float(breadth - 1) >= lim[inner, :], 1.0, 0.0)
        cel = cx[inner, breadth - 128:]
        old = act * shift_cols(s, 1) - cel * s
        new = act * shift_cols(s, 3) - cel * shift_cols(s, 2)
        keep = lane_f == 127
        sea0[inner, :] = jnp.where(keep, old, 0.0)
        sead[inner, :] = jnp.where(keep, new - old, 0.0)

    def substep(step, carry):
        for r0 in range(8, rows - 8, CH):
            sl = slice(r0, r0 + CH)
            e0 = e[sl, :]
            east = jnp.where(last, 0.0, shift_cols(e0, -1))
            nx = fxr[sl, :] * q[0, sl, :] - cx[sl, :] * (east - e0)
            ny = fyr[sl, :] * q[1, sl, :] - cy[sl, :] * (e[slice(r0 + 1, r0 + CH + 1), :] - e0)
            q[0, sl, :] = nx
            q[1, sl, :] = ny
            west = jnp.where(colc == 0, 0.0, shift_cols(nx, 1))
            north = q[1, slice(r0 - 1, r0 + CH - 1), :]
            e[sl, :] = e0 - DT_FINE * (nx - west + ny - north)
        return carry

    edge = slice(breadth - 128, breadth)
    inner = slice(8, rows - 8)

    def all_but_edge():
        er[...] = e[:, edge]
        qr[...] = q[:, :, edge]
        lax.fori_loop(0, SUBSTEPS, substep, 0)

    def edge_columns():
        for n in range(SUBSTEPS):
            w = (n + 0.5) / SUBSTEPS
            e0 = er[inner, :]
            east = jnp.where(lane_f == 127, 0.0, shift_cols(e0, -1))
            sea = sea0[inner, :] + w * sead[inner, :]
            nx = fxr[inner, edge] * qr[0, inner, :] - cx[inner, edge] * (east - e0) + sea
            ny = fyr[inner, edge] * qr[1, inner, :] - cy[inner, edge] * (er[9:rows - 7, :] - e0)
            qr[0, inner, :] = nx
            qr[1, inner, :] = ny
            north = qr[1, 7:rows - 9, :]
            er[inner, :] = e0 - DT_FINE * (nx - shift_cols(nx, 1) + ny - north)
        keep = lane_f >= 64
        e[inner, edge] = jnp.where(keep, er[inner, :], e[inner, edge])
        for i in range(2):
            q[i, inner, edge] = jnp.where(keep, qr[i, inner, :], q[i, inner, edge])

    def restrict(with_count):
        colf = iota((height, breadth), 1).astype(jnp.float32)
        wet = colf >= jnp.concatenate([lim[mid, :]] * reps, axis=1)
        act = jnp.where(wet, 1.0, 0.0)
        part = [
            mm(rowsum, act.astype(jnp.bfloat16)),
            left_hot(rowsum, act * e[mid, :], 2),
            left_hot(rowsum, q[0, mid, :], 2),
            left_hot(rowsum, q[1, mid, :], 2),
        ]
        if not with_count:
            part = part[1:]
        return right_hot(jnp.concatenate(part, axis=0), colsum, 2)

    all_but_edge()

    prow = iota((32, height), 0)
    rowsum = hot_of(prow == offset + fdiv5(iota((32, height), 1)))
    colsum = hot_of(fdiv5(iota((breadth, 128), 0)) == iota((breadth, 128), 1))
    j128 = iota((128, 128), 0)
    l128 = iota((128, 128), 1) & 31
    pick_same = hot_of(j128 == WIN + l128)
    pick_other = hot_of(j128 == col_b - col_a + WIN + l128)
    place_a = hot_of(iota((128, pc), 1) == col_a + iota((128, pc), 0))
    place_b = hot_of(iota((128, pc), 1) == col_b + iota((128, pc), 0))
    spread = hot_of(
        iota((rows - 16, 4 * ph), 1)
        == ph + offset + fdiv5(iota((rows - 16, 4 * ph), 0) + 32) - 8
    )

    for c in windows:
        c.arrive()
    wrow = (t - 1) * ph + iota((4 * ph, 128), 0)
    wcol = col_a + WIN + iota((4 * ph, 128), 1)
    w_row_open = jnp.where((wrow >= 0) & (wrow < ph * T - 1), 1.0, 0.0)
    w_col_open = jnp.where(wcol < pc - 1, 1.0, 0.0)
    b0 = pwb[0]
    b1 = pwb[1]
    we, wux, wuy, wd = b0, shift_cols(b0, -32), shift_cols(b0, -64), shift_cols(b0, -96)
    wwx, wwy = b1, shift_cols(b1, -32)
    whx = 0.5 * (wd + shift_cols(wd, -1))
    why = 0.5 * (wd + shift_rows(wd, -1))

    n1e, n1x, n1y = window_step(we, wux, wuy)
    set_sea(we, wux, n1e, n1x)
    edge_columns()

    s1 = restrict(True)
    glane = iota((32, 128), 1) >> 5

    def packed(pick):
        res = right_hot(s1, pick, 2)
        out = res[0:32]
        for i in range(1, 4):
            out = jnp.where(glane == i, res[32 * i:32 * (i + 1)], out)
        return out

    pks[0] = packed(pick_same)
    pks[1] = packed(pick_other)
    round_b = []
    n = 0
    for nest, src, ds in ((ko, 1, (0, 1, -1, 2, -2)), (k, 0, (1, -1))):
        for d in ds:
            round_b.append(Push(pks.at[src], pkb.at[n], sb.at[n], rb.at[n], nest, d))
            n += 1
    for c in round_b:
        c.start()

    def full_pushes(src, dst, s_sem, r_sem):
        return [
            Push(src.at[:, 0:ph, :], dst.at[0], s_sem.at[0], r_sem.at[0], ko, 0),
            Push(src.at[:, ph:2 * ph, :], dst.at[1], s_sem.at[1], r_sem.at[1], k, 1),
            Push(src.at[:, ph:2 * ph, :], dst.at[2], s_sem.at[2], r_sem.at[2], ko, 1),
        ]

    for i in range(4):
        ss1[i] = s1[32 * i:32 * (i + 1)]
    round_c = full_pushes(ss1, fs1, sc, rc)
    for c in round_c:
        c.start()

    all_but_edge()

    for c in parent_halo:
        c.arrive()
    xn = 16 + ph
    grow = t * ph - 8 + iota((xn, pc), 0)
    row_open = jnp.where((grow >= 0) & (grow < ph * T - 1), 1.0, 0.0)
    gcol = iota((ph, pc), 1)
    col_open = jnp.where(gcol < pc - 1, 1.0, 0.0)
    xd = xdep[...]
    hy_p = 0.5 * (xd + shift_rows(xd, -1))
    d_own = pdep
    hx_p = 0.5 * (d_own + shift_cols(d_own, -1))

    def tile_step(xe, xu, ux):
        ny = row_open * (xu - CP * hy_p * (shift_rows(xe, -1) - xe) + DT_COARSE * xwy[...]) * RP
        eo = xe[8:8 + ph]
        nx = col_open * (ux - CP * hx_p * (shift_cols(eo, -1) - eo) + DT_COARSE * wv[0]) * RP
        west = jnp.where(gcol == 0, 0.0, shift_cols(nx, 1))
        north = shift_rows(ny, 1)[8:8 + ph]
        nyo = ny[8:8 + ph]
        return eo - CP * (nx - west + nyo - north), nx, nyo

    t1e, t1x, t1y = tile_step(xlev[...], xuy[...], pfv[0])

    for c in round_c:
        c.arrive()

    def spread_sums(own_top, fs, comps):
        mine = jnp.concatenate([own_top[i] + fs[1, i] for i in range(comps)], axis=0)
        theirs = jnp.concatenate([fs[0, i] + fs[2, i] for i in range(comps)], axis=0)
        both = right_hot(mine, place_a, 2) + right_hot(theirs, place_b, 2)
        both = both * (1.0 / (RATIO * RATIO))
        return [both[i * ph:(i + 1) * ph] for i in range(comps)]

    g = spread_sums([s1[32 * i:32 * i + ph] for i in range(4)], fs1, 4)
    retained = 1.0 - g[0]
    t1e = t1e * retained + g[1]
    t1x = t1x * retained + g[2]
    t1y = t1y * retained + g[3]
    p2s[0] = t1e
    p2s[1] = t1y
    round_d = [
        Push(p2s.at[:, ph - 8:ph, :], p2b.at[0], sd.at[0], rd.at[0], k, 1),
        Push(p2s.at[:, 0:8, :], p2b.at[1], sd.at[1], rd.at[1], k, -1),
    ]
    for c in round_d:
        c.start()
    for c in round_b:
        c.arrive()
    zero16 = jnp.zeros((ph, 128), jnp.float32)
    near = pkb[0] + pks[0]
    prev = pkb[1] + pkb[5]
    nxt = pkb[2] + pkb[6]
    sums = jnp.concatenate([
        prev[0:ph] + pkb[3][ph:2 * ph],
        near[0:ph] + prev[ph:2 * ph],
        nxt[0:ph] + near[ph:2 * ph],
        pkb[4][0:ph] + nxt[ph:2 * ph],
    ], axis=0) * (1.0 / (RATIO * RATIO))
    keep = 1.0 - sums
    u1e = n1e * keep + shift_cols(sums, -32)
    u1x = n1x * keep + shift_cols(sums, -64)
    u1y = n1y * keep + shift_cols(sums, -96)
    n2e, n2x, _ = window_step(u1e, u1x, u1y)
    set_sea(u1e, u1x, n2e, n2x)
    edge_columns()

    s2 = restrict(False)
    for i in range(3):
        ss2[i] = s2[32 * i:32 * (i + 1)]
    round_e = full_pushes(ss2, fs2, se, re_)
    for c in round_e:
        c.start()
    fl_out[0] = e[mid, :]
    ff_out[0] = q[:, mid, :]
    for c in round_d:
        c.arrive()
    t2e, t2x, t2y = tile_step(
        jnp.concatenate([p2b[0, 0], t1e, p2b[1, 0]], axis=0),
        jnp.concatenate([p2b[0, 1], t1y, p2b[1, 1]], axis=0),
        t1x,
    )
    for c in round_e:
        c.arrive()
    g = spread_sums([s2[32 * i:32 * i + ph] for i in range(3)], fs2, 3)
    pl_out[...] = t2e * retained + g[0]
    pf_out[0] = t2x * retained + g[1]
    pf_out[1] = t2y * retained + g[2]
    for c in round_a + round_b + round_c + round_d + round_e:
        c.sent()


def store(*refs):
    outs = [pltpu.make_async_copy(refs[i], refs[4 + i], refs[8].at[i]) for i in range(4)]
    for i in (1, 0, 3, 2):
        outs[i].start()
    for c in outs:
        c.wait()


def on_device(fl, ff, fd, shore, ext, inter, plev, pflux, pdep, wind):
    _, height, breadth = fl.shape
    ph, pc = plev.shape
    T = lax.axis_size("tile")
    rows = height + 32
    f32 = jnp.float32
    fine = pltpu.VMEM((rows, breadth), f32)
    strip = pltpu.VMEM((rows, 128), f32)
    ext_p = pltpu.VMEM((ph + 16, pc), f32)
    dma = pltpu.SemaphoreType.DMA
    vm = pl.BlockSpec(memory_space=pltpu.VMEM)
    hb = pl.BlockSpec(memory_space=pltpu.HBM)
    outs = pl.pallas_call(
        functools.partial(kernel, T, height, breadth, ph, pc),
        out_shape=[pltpu.VMEM(x.shape, f32) for x in (fl, ff, plev, pflux)],
        in_specs=[hb] * 10,
        out_specs=[vm] * 4,
        scratch_shapes=[
            fine, pltpu.VMEM((2, rows, breadth), f32), fine, strip,
            fine, fine, fine, fine, strip, strip, strip, pltpu.VMEM((2, rows, 128), f32),
            pltpu.VMEM((2, ph, pc), f32), pltpu.VMEM((2, ph, pc), f32),
            pltpu.VMEM((1, height), jnp.int32), pltpu.SMEM((1, 1), jnp.int32), pltpu.SMEM((2, 2), jnp.int32),
            ext_p, ext_p, ext_p, ext_p,
            pltpu.VMEM((2, ph, 128), f32), pltpu.VMEM((2, 4 * ph, 128), f32),
            pltpu.VMEM((2, 2 * ph, 128), f32), pltpu.VMEM((7, 2 * ph, 128), f32),
            pltpu.VMEM((4, 2 * ph, 128), f32), pltpu.VMEM((3, 4, ph, 128), f32),
            pltpu.VMEM((3, 2 * ph, 128), f32), pltpu.VMEM((3, 3, ph, 128), f32),
            pltpu.VMEM((2, ph, pc), f32), pltpu.VMEM((2, 2, 8, pc), f32),
            dma((19,)), dma((19,)), dma((7,)), dma((7,)), dma((3,)), dma((3,)),
            dma((2,)), dma((2,)), dma((3,)), dma((3,)), dma((10,)),
        ],
        compiler_params=pltpu.CompilerParams(
            collective_id=0, has_side_effects=True, vmem_limit_bytes=48 * 1024 * 1024),
        name="nested",
    )(*[pltpu.with_memory_space_constraint(x, pltpu.HBM) if x is not ext else x for x in (fl, ff, fd, shore, ext, inter, plev, pflux, pdep, wind)])
    return pl.pallas_call(
        store,
        out_shape=[jax.ShapeDtypeStruct(x.shape, f32) for x in (fl, ff, plev, pflux)],
        in_specs=[vm] * 4,
        out_specs=[hb] * 4,
        scratch_shapes=[dma((4,))],
        compiler_params=pltpu.CompilerParams(vmem_limit_bytes=48 * 1024 * 1024),
        name="store",
    )(*outs)


def solution(mesh):
    in_specs = (
        P("nest", "tile", None),
        P("nest", None, "tile", None),
        P("nest", "tile", None),
        P("nest", "tile"),
        P("nest", "tile"),
        P(),
        P("tile", None),
        P(None, "tile", None),
        P("tile", None),
        P(None, "tile", None),
    )
    out_specs = (
        P("nest", "tile", None),
        P("nest", None, "tile", None),
        P("tile", None),
        P(None, "tile", None),
    )
    return jax.shard_map(
        on_device, mesh=mesh, in_specs=in_specs, out_specs=out_specs, check_vma=False
    )
```

profile of v0, /device:TPU:21, one launch (start us, length us, event | category | flops | bytes accessed | tf_op | source)
XLA Modules:
  0.0 23.8 jit_solution(7904689767418929856)
XLA Ops:
  1.3 21.6 %nested.1 = (f32[1,80,640]{2,1,0:T(8,128)S(1)}, f32[1,2,80,640]{3,2,1,0:T(8,128)S(1)}, f32[16,512]{1,0:T(8,128)S(1)}, f32[2,16,512]{2,1,0:T(8,128)S(1)}) custom-call(f32[1,80,640]{2,1,0:T(8,128)} %fl.1, f32[1,2,80,640]{3,2,1,0:T(8,128)} %ff.1, f32[1,80,640]{2,1,0:T(8,128)} %fd.1, s32[1,80]{1,0:T(1,128)} %shore.1, s32[1,1]{1,0:T(1,128)S(6)} %copy.14.ext, ...), custom_call_target="tpu_custom_call" | custom-call | tf_op jit(solution)/shard_map/nested/pallas_call | solution.py:507
  22.9 0.9 %store.1 = (f32[1,80,640]{2,1,0:T(8,128)}, f32[1,2,80,640]{3,2,1,0:T(8,128)}, f32[16,512]{1,0:T(8,128)}, f32[2,16,512]{2,1,0:T(8,128)}) custom-call(f32[1,80,640]{2,1,0:T(8,128)S(1)} %get-tuple-element.8.refs_0_, f32[1,2,80,640]{3,2,1,0:T(8,128)S(1)} %get-tuple-element.9.refs_1_, f32[16,512]{1,0:T(8,128)S(1)} %get-tuple-element.10.refs_2_, ...), custom_call_target="tpu_custom_call" | custom-call | tf_op jit(solution)/shard_map/store/pallas_call | solution.py:530
where the time goes:
time: 23.9 us; the launch traced here: 23.8 us
  Pallas kernels  22.5 us (94%)
  between operations  1.29 us (5%)
    pallas_call x1, Pallas kernels, on_device(): pl.pallas_call(functools.partial(kernel, T, height, breadth, ph, pc), out...  21.6 us
    pallas_call x1, Pallas kernels, on_device(): pl.pallas_call(store, out_shape=[jax.ShapeDtypeStruct(x.shape, f32) for x...  0.88 us

commit v1 on v0

v1 whole, which is shorter than its diff:
```python
import functools

import jax
import jax.numpy as jnp
from jax import lax
from jax.experimental import pallas as pl
from jax.experimental.pallas import tpu as pltpu
from jax.sharding import PartitionSpec as P

RATIO = 5
SUBSTEPS = 4
DT_FINE = 0.4
DT_COARSE = 1.6
DX_COARSE = 5.0
FRICTION = 0.05
RF = 1.0 / (1.0 + DT_FINE * FRICTION)
RP = 1.0 / (1.0 + DT_COARSE * FRICTION)
CP = DT_COARSE / DX_COARSE
FAR = 1.0e6
WIN = 112
CH = 16


def parts_of(x, n):
    out = []
    for _ in range(n):
        hi = x.astype(jnp.bfloat16)
        out.append(hi)
        x = x - hi.astype(jnp.float32)
    return out


def mm(a, b):
    return lax.dot_general(a, b, (((1,), (0,)), ((), ())), preferred_element_type=jnp.float32)


def left_hot(hot, x, n):
    return sum(mm(hot, p) for p in parts_of(x, n))


def right_hot(x, hot, n):
    return sum(mm(p, hot) for p in parts_of(x, n))


def hot_of(mask):
    return jnp.where(mask, 1.0, 0.0).astype(jnp.bfloat16)


def iota(shape, axis):
    return lax.broadcasted_iota(jnp.int32, shape, axis)


def fdiv5(x):
    return jnp.floor((x.astype(jnp.float32) + 0.5) * 0.2).astype(jnp.int32)


def shift_rows(x, by):
    return pltpu.roll(x, by % x.shape[0], 0)


def shift_cols(x, by):
    return pltpu.roll(x, by % x.shape[1], 1)


def parent_step(e, ux, uy, hx, hy, wx, wy, col_open, row_open):
    nx = col_open * (ux - CP * hx * (shift_cols(e, -1) - e) + DT_COARSE * wx) * RP
    ny = row_open * (uy - CP * hy * (shift_rows(e, -1) - e) + DT_COARSE * wy) * RP
    return nx, ny


def kernel(
    T, height, breadth, ph, pc,
    fl, ff, fd, shore, ext, inter, plev_h, pflux_h, pdep_h, wind_h,
    fl_out, ff_out, pl_out, pf_out,
    e, q, dep, lim, fxr, cx, fyr, cy, sea0, sead, er, qr, be, bq,
    plv, pfv, pdv, wv, shv, exs, ins, pws, pwb, hs, hr, pks, pkb,
    cs, c0a, c0b, c1, es, e0a, e0b, e1, gs, g0a, g0b, g1,
    ssem, rsem, lsem,
):
    k = lax.axis_index("nest")
    t = lax.axis_index("tile")
    ko = 1 - k
    top = 16
    rows = height + 32
    mid = slice(top, top + height)
    inner = slice(8, rows - 8)
    edge = slice(breadth - 128, breadth)
    halo_n = slice(top - 8, top)
    halo_s = slice(top + height, top + height + 8)

    def have(d):
        return (t + d >= 0) & (t + d < T)

    locals_ = [
        pltpu.make_async_copy(src, dst, lsem.at[i])
        for i, (src, dst) in enumerate((
            (shore, shv), (ext, exs), (inter, ins),
            (plev_h, plv), (pflux_h, pfv), (pdep_h, pdv), (wind_h, wv),
            (fd.at[0], dep.at[mid, :]), (fl.at[0], e.at[mid, :]), (ff.at[0], q.at[:, mid, :]),
        ))
    ]
    for c in locals_:
        c.start()

    for buf in (pwb, pkb, c0a, c0b, c1, e0a, e0b, e1, g0a, g0b, g1, hr):
        buf[...] = jnp.zeros(buf.shape, jnp.float32)
    zrow = jnp.zeros((8, breadth), jnp.float32)
    far = jnp.full((8, 128), FAR, jnp.float32)
    for missing, s, b, bs in ((-1, halo_n, 0, slice(8, 16)), (1, halo_s, 1, slice(24, 32))):
        @pl.when(jnp.logical_not(have(missing)))
        def _():
            dep[s, :] = zrow
            lim[s, :] = far
            be[b, bs, :] = zrow
            bq[b, 0, bs, :] = zrow
            bq[b, 1, bs, :] = zrow

    barrier = pltpu.get_barrier_semaphore()

    def greet(nest, d, only=None):
        ok = have(d)
        if only is not None:
            ok = ok & (k == only)

        @pl.when(ok)
        def _():
            pl.semaphore_signal(barrier, inc=1, device_id=(nest, t + d), device_id_type=pl.DeviceIdType.MESH)

    def expect(d, only=None):
        ok = have(d)
        if only is not None:
            ok = ok & (k == only)
        return ok.astype(jnp.int32)

    for d in (1, -1):
        greet(k, d)
    greet(ko, 0)
    greet(ko, -1)
    greet(k, 2, 0)
    greet(ko, 1, 0)
    greet(ko, 2, 0)
    greet(ko, -2, 1)
    count = (expect(1) + expect(-1) + 1 + expect(1) + expect(-2, 0) + expect(2, 0)
             + expect(-1, 1) + expect(-2, 1))

    pushes = []

    class Push:
        def __init__(self, src, dst, same, d, only=None):
            n = len(pushes)
            pushes.append(self)
            self.go, self.come = have(d), have(-d)
            if only is not None:
                self.go = self.go & (k == only)
                self.come = self.come & (k == (only if same else 1 - only))
            self.c = pltpu.make_async_remote_copy(
                src_ref=src, dst_ref=dst, send_sem=ssem.at[n], recv_sem=rsem.at[n],
                device_id=(k if same else ko, t + d), device_id_type=pl.DeviceIdType.MESH)

        def start(self):
            pl.when(self.go)(lambda: self.c.start())

        def sent(self):
            pl.when(self.go)(lambda: self.c.wait_send())

        def arrive(self):
            pl.when(self.come)(lambda: self.c.wait_recv())

    def start(group):
        for c in group:
            c.start()
        return group

    def arrive(group):
        for c in group:
            c.arrive()

    pl.semaphore_wait(barrier, count)
    halo = []
    for d in (1, -1):
        own = slice(height - 8, height) if d == 1 else slice(0, 8)
        to = halo_n if d == 1 else halo_s
        b, bs = (0, slice(8, 16)) if d == 1 else (1, slice(24, 32))
        halo += [
            Push(fd.at[0, own, :], dep.at[to, :], True, d),
            Push(fl.at[0, own, :], be.at[b, bs, :], True, d),
            Push(ff.at[0, :, own, :], bq.at[b, :, bs, :], True, d),
        ]
    start(halo)

    for c in locals_[:3]:
        c.wait()
    offset = jnp.where(k == 0, ins[0, 0], ins[1, 0])
    col_a = jnp.where(k == 0, ins[0, 1], ins[1, 1])
    col_b = jnp.where(k == 0, ins[1, 1], ins[0, 1])

    diag = iota((height, height), 0) == iota((height, height), 1)
    limit = jnp.sum(jnp.where(diag, shv[...].astype(jnp.float32), 0.0), axis=1, keepdims=True)
    r = iota((height, 128), 0)
    live = (r < exs[0, 0]) & (offset + t * (height // RATIO) + fdiv5(r) < ph * T)
    lim[mid, :] = jnp.where(live, limit, FAR)
    limits = [
        Push(lim.at[top + height - 8:top + height, :], lim.at[halo_n, :], True, 1),
        Push(lim.at[top:top + 8, :], lim.at[halo_s, :], True, -1),
    ]
    start(limits)

    take = hot_of(iota((pc, 128), 0) == col_a + WIN + (iota((pc, 128), 1) & 31))
    for c in locals_[3:7]:
        c.wait()
    parent = [plv[...], pdv[...], pfv[1], pfv[0], wv[0], wv[1]]
    stack = jnp.concatenate([parent[0], parent[3], parent[2], parent[1], parent[4], parent[5]], axis=0)
    win = right_hot(stack, take, 3)
    group = iota((ph, 128), 1) >> 5
    pack0 = jnp.zeros((ph, 128), jnp.float32)
    pack1 = jnp.zeros((ph, 128), jnp.float32)
    for i in range(4):
        pack0 = jnp.where(group == i, win[i * ph:(i + 1) * ph], pack0)
    for i in range(2):
        pack1 = jnp.where(group == i, win[(4 + i) * ph:(5 + i) * ph], pack1)
    pws[0] = pack0
    pws[1] = pack1
    windows = [
        Push(pws.at[:, 8:ph, :], pwb.at[:, 8:ph, :], True, 1),
        Push(pws.at[:, :, :], pwb.at[:, 2 * ph:3 * ph, :], True, -1),
        Push(pws.at[:, 0:8, :], pwb.at[:, 3 * ph:3 * ph + 8, :], True, -2, 0),
    ]
    start(windows)
    pwb[:, ph:2 * ph, :] = pws[...]

    pair = iota((8, pc), 0) >> 1
    for at, tile, first in ((0, slice(ph - 8, ph), 2), (1, slice(0, 8), 0)):
        for part, members in ((0, parent[:4]), (1, parent[4:])):
            out = jnp.zeros((8, pc), jnp.float32)
            for i, x in enumerate(members):
                out = jnp.where(pair == i, shift_rows(x[tile], 2 * i + first), out)
            hs[at, 8 * part:8 * part + 8, :] = out
    parent_halo = [
        Push(hs.at[0], hr.at[0], True, 1),
        Push(hs.at[1], hr.at[1], True, -1),
    ]
    start(parent_halo)

    for s in (slice(0, 8), slice(rows - 8, rows)):
        e[s, :] = zrow
        dep[s, :] = zrow
        q[0, s, :] = zrow
        q[1, s, :] = zrow
        lim[s, :] = far
        er[s, :] = zrow[:, :128]
        qr[0, s, :] = zrow[:, :128]
        qr[1, s, :] = zrow[:, :128]
    for b in range(2):
        for s in (slice(0, 8), slice(32, 40)):
            be[b, s, :] = zrow
            bq[b, 1, s, :] = zrow

    colc = iota((CH, breadth), 1)
    last = colc == breadth - 1
    reps = breadth // 128

    def coefficients(r0):
        sl = slice(r0, r0 + CH)
        ss = slice(r0 + 1, r0 + CH + 1)
        colf = colc.astype(jnp.float32)
        wide = lambda s: jnp.concatenate([lim[s, :]] * reps, axis=1)
        act = jnp.where(colf >= wide(sl), 1.0, 0.0)
        act_s = jnp.where(colf >= wide(ss), 1.0, 0.0)
        d0 = dep[sl, :]
        fx = jnp.where(last, 0.0, act * shift_cols(act, -1))
        fxr[sl, :] = fx * RF
        cx[sl, :] = jnp.where(
            last, act * jnp.sqrt(d0), (DT_FINE * RF * 0.5) * fx * (d0 + shift_cols(d0, -1)))
        fy = act * act_s
        fyr[sl, :] = fy * RF
        cy[sl, :] = (DT_FINE * RF * 0.5) * fy * (d0 + dep[ss, :])

    def advance(ef, qf, r0, n, off):
        sl = slice(r0, r0 + n)
        co = slice(r0 + off, r0 + off + n)
        col = iota((n, breadth), 1)
        e0 = ef[sl, :]
        east = jnp.where(col == breadth - 1, 0.0, shift_cols(e0, -1))
        nx = fxr[co, :] * qf[0, sl, :] - cx[co, :] * (east - e0)
        ny = fyr[co, :] * qf[1, sl, :] - cy[co, :] * (ef[r0 + 1:r0 + n + 1, :] - e0)
        qf[0, sl, :] = nx
        qf[1, sl, :] = ny
        west = jnp.where(col == 0, 0.0, shift_cols(nx, 1))
        north = qf[1, r0 - 1:r0 + n - 1, :]
        ef[sl, :] = e0 - DT_FINE * (nx - west + ny - north)

    locals_[7].wait()
    for r0 in range(8 + CH, rows - 8 - CH, CH):
        coefficients(r0)
    for c in locals_[8:]:
        c.wait()
    be[0, 16:32, :] = e[top:top + 16, :]
    be[1, 8:24, :] = e[top + height - 16:top + height, :]
    er[mid, :] = e[mid, edge]
    for i in range(2):
        bq[0, i, 16:32, :] = q[i, top:top + 16, :]
        bq[1, i, 8:24, :] = q[i, top + height - 16:top + height, :]
        qr[i, mid, :] = q[i, mid, edge]

    def inside(step, carry):
        for r0 in range(8 + CH, rows - 8 - CH, CH):
            advance(e, q, r0, CH, 0)
        return carry

    lax.fori_loop(0, SUBSTEPS, inside, 0)

    lane = iota((4 * ph, 128), 1)
    lane_f = iota((rows - 16, 128), 1)
    lev_at = 128 - WIN
    flux_at = 127 - WIN
    rowsum = hot_of(iota((32, height), 0) == offset + fdiv5(iota((32, height), 1)))
    l32 = iota((128, 128), 1) & 31
    sum_same = hot_of(fdiv5(iota((128, 128), 0) + (breadth - 128)) == WIN + l32)
    begin = 0
    for s in range(128, breadth - 255, 128):
        begin = jnp.where(RATIO * (col_b - col_a + 127) >= s, s, begin)
    sum_other = hot_of(
        fdiv5(iota((256, 128), 0) + begin) == col_b - col_a + WIN + (iota((256, 128), 1) & 31))
    spread = hot_of(
        iota((rows - 16, 4 * ph), 1)
        == ph + offset + fdiv5(iota((rows - 16, 4 * ph), 0) + 32) - 8
    )
    wrow = (t - 1) * ph + iota((4 * ph, 128), 0)
    wcol = col_a + WIN + iota((4 * ph, 128), 1)
    w_row_open = jnp.where((wrow >= 0) & (wrow < ph * T - 1), 1.0, 0.0)
    w_col_open = jnp.where(wcol < pc - 1, 1.0, 0.0)

    arrive(halo)
    arrive(limits)
    arrive(windows)

    er[halo_n, :] = be[0, 8:16, edge]
    er[halo_s, :] = be[1, 24:32, edge]
    for i in range(2):
        qr[i, halo_n, :] = bq[0, i, 8:16, edge]
        qr[i, halo_s, :] = bq[1, i, 24:32, edge]
    coefficients(8)
    coefficients(rows - 8 - CH)

    b0 = pwb[0]
    b1 = pwb[1]
    we, wux, wuy, wd = b0, shift_cols(b0, -32), shift_cols(b0, -64), shift_cols(b0, -96)
    wwx, wwy = b1, shift_cols(b1, -32)
    whx = 0.5 * (wd + shift_cols(wd, -1))
    why = 0.5 * (wd + shift_rows(wd, -1))

    def window_step(we, wux, wuy):
        nx, ny = parent_step(we, wux, wuy, whx, why, wwx, wwy, w_col_open, w_row_open)
        ne = we - CP * (nx - shift_cols(nx, 1) + ny - shift_rows(ny, 1))
        return ne, nx, ny

    def set_sea(oe, oux, ne, nux):
        z = jnp.where(lane == 127, shift_cols(oe, 127 - lev_at), 0.0)
        z = jnp.where(lane == 126, shift_cols(oux, 126 - flux_at), z)
        z = jnp.where(lane == 125, shift_cols(ne, 125 - lev_at), z)
        z = jnp.where(lane == 124, shift_cols(nux, 124 - flux_at), z)
        s = left_hot(spread, z, 3)
        act = jnp.where(float(breadth - 1) >= lim[inner, :], 1.0, 0.0)
        cel = cx[inner, breadth - 128:]
        old = act * shift_cols(s, 1) - cel * s
        new = act * shift_cols(s, 3) - cel * shift_cols(s, 2)
        keep = lane_f == 127
        sea0[inner, :] = jnp.where(keep, old, 0.0)
        sead[inner, :] = jnp.where(keep, new - old, 0.0)

    def edge_columns():
        for n in range(SUBSTEPS):
            w = (n + 0.5) / SUBSTEPS
            e0 = er[inner, :]
            east = jnp.where(lane_f == 127, 0.0, shift_cols(e0, -1))
            sea = sea0[inner, :] + w * sead[inner, :]
            nx = fxr[inner, edge] * qr[0, inner, :] - cx[inner, edge] * (east - e0) + sea
            ny = fyr[inner, edge] * qr[1, inner, :] - cy[inner, edge] * (er[9:rows - 7, :] - e0)
            qr[0, inner, :] = nx
            qr[1, inner, :] = ny
            north = qr[1, 7:rows - 9, :]
            er[inner, :] = e0 - DT_FINE * (nx - shift_cols(nx, 1) + ny - north)

    def merge_edge(where):
        n = where.stop - where.start
        keep = iota((n, 128), 1) >= 64
        e[where, edge] = jnp.where(keep, er[where, :], e[where, edge])
        for i in range(2):
            q[i, where, edge] = jnp.where(keep, qr[i, where, :], q[i, where, edge])

    for n in range(SUBSTEPS):
        for r0 in (8, 16, 24):
            advance(be.at[0], bq.at[0], r0, 8, 0)
            advance(be.at[1], bq.at[1], r0, 8, rows - 40)
    r8 = iota((8, breadth), 0)
    for dst, bnd in ((e, lambda b: be.at[b]), (q.at[0], lambda b: bq.at[b, 0]), (q.at[1], lambda b: bq.at[b, 1])):
        dst[8:24, :] = bnd(0)[8:24, :]
        dst[24:32, :] = jnp.where(r8 < 4, bnd(0)[24:32, :], dst[24:32, :])
        dst[rows - 32:rows - 24, :] = jnp.where(r8 >= 4, bnd(1)[8:16, :], dst[rows - 32:rows - 24, :])
        dst[rows - 24:rows - 8, :] = bnd(1)[16:32, :]

    n1e, n1x, n1y = window_step(we, wux, wuy)
    set_sea(we, wux, n1e, n1x)
    edge_columns()
    merge_edge(inner)

    glane = iota((32, 128), 1) >> 5

    def packed(res, n):
        out = res[0:32]
        for i in range(1, n):
            out = jnp.where(glane == i, res[32 * i:32 * (i + 1)], out)
        return out

    def wet(width, start):
        colf = (iota((height, width), 1) + start).astype(jnp.float32)
        return jnp.where(colf >= jnp.concatenate([lim[mid, :]] * (width // 128), axis=1), 1.0, 0.0)

    def restrict(act, lev, qx, qy, columns, with_count):
        part = [
            left_hot(rowsum, act * lev, 2),
            left_hot(rowsum, qx, 2),
            left_hot(rowsum, qy, 2),
        ]
        if with_count:
            part = [mm(rowsum, act.astype(jnp.bfloat16))] + part
        return right_hot(jnp.concatenate(part, axis=0), columns, 2)

    pks[0] = packed(restrict(wet(128, breadth - 128), er[mid, :], qr[0, mid, :], qr[1, mid, :], sum_same, True), 4)

    def there(ref):
        out = ref[mid, 0:256]
        for s in range(128, breadth - 255, 128):
            out = jnp.where(begin == s, ref[mid, s:s + 256], out)
        return out

    pks[1] = packed(restrict(wet(256, begin), there(e), there(q.at[0]), there(q.at[1]), sum_other, True), 4)
    near = start([
        Push(pks.at[1], pkb.at[0], False, 0),
        Push(pks.at[1, 8:32, :], pkb.at[1, 8:32, :], False, 1),
        Push(pks.at[1, 0:16, :], pkb.at[2, 0:16, :], False, -1, 1),
        Push(pks.at[1, 24:32, :], pkb.at[3, 24:32, :], False, 2, 0),
        Push(pks.at[1, 0:8, :], pkb.at[4, 0:8, :], False, -2, 1),
        Push(pks.at[0, 8:32, :], pkb.at[5, 8:32, :], True, 1),
        Push(pks.at[0, 0:24, :], pkb.at[6, 0:24, :], True, -1),
    ])

    colsum = hot_of(fdiv5(iota((breadth, 128), 0)) == iota((breadth, 128), 1))
    s1 = restrict(wet(breadth, 0), e[mid, :], q[0, mid, :], q[1, mid, :], colsum, True)
    for i in range(4):
        cs[i] = s1[32 * i:32 * (i + 1)]

    sums1 = start([
        Push(cs.at[:, 0:24, :], c0a.at[:, 8:32, :], False, 0, 0),
        Push(cs.at[:, 0:16, :], c1.at[:, 8:24, :], False, 0, 1),
        Push(cs.at[:, 8:32, :], c0b.at[:, 0:24, :], True, 1, 0),
        Push(cs.at[:, 8:32, :], c0b.at[:, 0:24, :], False, 1, 0),
        Push(cs.at[:, 8:16, :], c1.at[:, 0:8, :], True, 1, 1),
        Push(cs.at[:, 8:16, :], c1.at[:, 0:8, :], False, 1, 1),
        Push(cs.at[:, 0:8, :], c1.at[:, 24:32, :], True, -1, 1),
        Push(cs.at[:, 0:8, :], c1.at[:, 24:32, :], False, -1, 1),
    ])

    er[...] = e[:, edge]
    qr[...] = q[:, :, edge]

    def everywhere(step, carry):
        for r0 in range(8, rows - 8, CH):
            advance(e, q, r0, CH, 0)
        return carry

    lax.fori_loop(0, SUBSTEPS, everywhere, 0)

    bulk = hot_of((fdiv5(iota((breadth, 128), 0)) == iota((breadth, 128), 1)) & (iota((breadth, 128), 1) < breadth // RATIO - 1))
    s2 = restrict(wet(breadth, 0), e[mid, :], q[0, mid, :], q[1, mid, :], bulk, False)
    for i in range(3):
        es[i] = s2[32 * i:32 * (i + 1)]

    def final_sums(src, a0, b0, one, idx):
        return start([
            Push(src.at[idx(0)], a0, False, 0, 0),
            Push(src.at[idx(0)], one, False, 0, 1),
            Push(src.at[idx(1)], b0, True, 1, 0),
            Push(src.at[idx(1)], b0, False, 1, 0),
        ])

    sums2 = final_sums(es, e0a, e0b, e1, lambda i: (slice(None), slice(ph * i, ph * (i + 1)), slice(None)))

    xn = 16 + ph
    grow = t * ph - 8 + iota((xn, pc), 0)
    row_open = jnp.where((grow >= 0) & (grow < ph * T - 1), 1.0, 0.0)
    gcol = iota((xn, pc), 1)
    col_open = jnp.where(gcol < pc - 1, 1.0, 0.0)
    col_0 = jnp.where(k == 0, col_a, col_b)
    col_1 = jnp.where(k == 0, col_b, col_a)
    place_0 = hot_of(iota((128, pc), 1) == col_0 + iota((128, pc), 0))
    place_1 = hot_of(iota((128, pc), 1) == col_1 + iota((128, pc), 0))

    arrive(near)
    beside = pkb[0] + pks[0]
    prev = pkb[1] + pkb[5]
    nxt = pkb[2] + pkb[6]
    sums = jnp.concatenate([
        prev[0:ph] + pkb[3][ph:2 * ph],
        beside[0:ph] + prev[ph:2 * ph],
        nxt[0:ph] + beside[ph:2 * ph],
        pkb[4][0:ph] + nxt[ph:2 * ph],
    ], axis=0) * (1.0 / (RATIO * RATIO))
    keep = 1.0 - sums
    u1e = n1e * keep + shift_cols(sums, -32)
    u1x = n1x * keep + shift_cols(sums, -64)
    u1y = n1y * keep + shift_cols(sums, -96)
    n2e, n2x, _ = window_step(u1e, u1x, u1y)
    set_sea(u1e, u1x, n2e, n2x)
    edge_columns()

    sum_last = hot_of(iota((128, 128), 0) >= 128 - RATIO)
    gs[...] = packed(restrict(wet(128, breadth - 128), er[mid, :], qr[0, mid, :], qr[1, mid, :], sum_last, False), 3)
    sums3 = final_sums(gs, g0a, g0b, g1, lambda i: (slice(ph * i, ph * (i + 1)), slice(None)))

    merge_edge(mid)
    fl_out[0] = e[mid, :]
    ff_out[0] = q[:, mid, :]

    arrive(parent_halo)

    def extended(own, i):
        part, j = (0, i) if i < 4 else (8, i - 4)
        return jnp.concatenate([
            shift_rows(hr[0, part:part + 8, :], 6 - 2 * j), own, shift_rows(hr[1, part:part + 8, :], -2 * j)], axis=0)

    xe, xd, xuy, xux, xwx, xwy = [
        extended(x, i) for i, x in enumerate((plv[...], pdv[...], pfv[1], pfv[0], wv[0], wv[1]))]
    hx_p = 0.5 * (xd + shift_cols(xd, -1))
    hy_p = 0.5 * (xd + shift_rows(xd, -1))

    def tile_step(xe, ux, uy):
        nx, ny = parent_step(xe, ux, uy, hx_p, hy_p, xwx, xwy, col_open, row_open)
        west = jnp.where(gcol == 0, 0.0, shift_cols(nx, 1))
        return xe - CP * (nx - west + ny - shift_rows(ny, 1)), nx, ny

    t1e, t1x, t1y = tile_step(xe, xux, xuy)

    arrive(sums1)

    @pl.when(k == 0)
    def _():
        c0a[:, 8:32, :] = cs[:, 0:24, :]

    @pl.when(k == 1)
    def _():
        c1[:, 8:24, :] = cs[:, 0:16, :]

    def spread_sums(a0, b0, one, comps):
        nest0 = jnp.concatenate([a0[i] + b0[i] for i in range(comps)], axis=0)
        nest1 = jnp.concatenate([one[i] for i in range(comps)], axis=0)
        both = right_hot(nest0, place_0, 2) + right_hot(nest1, place_1, 2)
        both = both * (1.0 / (RATIO * RATIO))
        n = both.shape[0] // comps
        return [both[i * n:(i + 1) * n] for i in range(comps)]

    g = spread_sums(c0a, c0b, c1, 4)
    retained = 1.0 - g[0]
    t2 = tile_step(t1e * retained + g[1], t1x * retained + g[2], t1y * retained + g[3])
    own_p = slice(8, 8 + ph)
    held = retained[own_p]

    arrive(sums2)

    @pl.when(k == 0)
    def _():
        e0a[...] = es[:, 0:ph, :]
        g0a[...] = gs[0:ph, :]

    @pl.when(k == 1)
    def _():
        e1[...] = es[:, 0:ph, :]
        g1[...] = gs[0:ph, :]

    g = spread_sums(e0a, e0b, e1, 3)
    base = [t2[i][own_p] * held + g[i] for i in range(3)]
    at_0 = gcol[own_p] == col_0 + (breadth // RATIO - 1)
    at_1 = gcol[own_p] == col_1 + (breadth // RATIO - 1)
    arrive(sums3)
    z0 = (g0a[...] + g0b[...]) * (1.0 / (RATIO * RATIO))
    z1 = g1[...] * (1.0 / (RATIO * RATIO))
    outs = []
    for i in range(3):
        v0 = jnp.broadcast_to(z0[:, 32 * i:32 * i + 1], (ph, pc))
        v1 = jnp.broadcast_to(z1[:, 32 * i:32 * i + 1], (ph, pc))
        outs.append(base[i] + jnp.where(at_0, v0, 0.0) + jnp.where(at_1, v1, 0.0))
    pl_out[...] = outs[0]
    pf_out[0] = outs[1]
    pf_out[1] = outs[2]
    for c in pushes:
        c.sent()


def store(*refs):
    outs = [pltpu.make_async_copy(refs[i], refs[4 + i], refs[8].at[i]) for i in range(4)]
    for i in (1, 0, 3, 2):
        outs[i].start()
    for c in outs:
        c.wait()


def on_device(fl, ff, fd, shore, ext, inter, plev, pflux, pdep, wind):
    _, height, breadth = fl.shape
    ph, pc = plev.shape
    T = lax.axis_size("tile")
    rows = height + 32
    f32 = jnp.float32

    def vmem(*shape):
        return pltpu.VMEM(shape, f32)

    fine, strip = vmem(rows, breadth), vmem(rows, 128)
    dma = pltpu.SemaphoreType.DMA
    vm = pl.BlockSpec(memory_space=pltpu.VMEM)
    hb = pl.BlockSpec(memory_space=pltpu.HBM)
    pin = lambda x: pltpu.with_memory_space_constraint(x, pltpu.HBM)
    outs = pl.pallas_call(
        functools.partial(kernel, T, height, breadth, ph, pc),
        out_shape=[pltpu.VMEM(x.shape, f32) for x in (fl, ff, plev, pflux)],
        in_specs=[hb] * 10,
        out_specs=[vm] * 4,
        scratch_shapes=[
            fine, vmem(2, rows, breadth), fine, strip,
            fine, fine, fine, fine, strip, strip, strip, vmem(2, rows, 128),
            vmem(2, 40, breadth), vmem(2, 2, 40, breadth),
            vmem(ph, pc), vmem(2, ph, pc), vmem(ph, pc), vmem(2, ph, pc),
            pltpu.VMEM((1, height), jnp.int32), pltpu.SMEM((1, 1), jnp.int32), pltpu.SMEM((2, 2), jnp.int32),
            vmem(2, ph, 128), vmem(2, 4 * ph, 128), vmem(2, 16, pc), vmem(2, 16, pc),
            vmem(2, 2 * ph, 128), vmem(7, 2 * ph, 128),
            vmem(4, 2 * ph, 128), vmem(4, 2 * ph, 128), vmem(4, 2 * ph, 128), vmem(4, 2 * ph, 128),
            vmem(3, 2 * ph, 128), vmem(3, ph, 128), vmem(3, ph, 128), vmem(3, ph, 128),
            vmem(2 * ph, 128), vmem(ph, 128), vmem(ph, 128), vmem(ph, 128),
            dma((36,)), dma((36,)), dma((10,)),
        ],
        compiler_params=pltpu.CompilerParams(
            collective_id=0, has_side_effects=True, vmem_limit_bytes=48 * 1024 * 1024),
        name="nested",
    )(pin(fl), pin(ff), pin(fd), pin(shore), ext, pin(inter), pin(plev), pin(pflux), pin(pdep), pin(wind))
    return pl.pallas_call(
        store,
        out_shape=[jax.ShapeDtypeStruct(x.shape, f32) for x in (fl, ff, plev, pflux)],
        in_specs=[vm] * 4,
        out_specs=[hb] * 4,
        scratch_shapes=[dma((4,))],
        compiler_params=pltpu.CompilerParams(vmem_limit_bytes=48 * 1024 * 1024),
        name="store",
    )(*outs)


def solution(mesh):
    in_specs = (
        P("nest", "tile", None),
        P("nest", None, "tile", None),
        P("nest", "tile", None),
        P("nest", "tile"),
        P("nest", "tile"),
        P(),
        P("tile", None),
        P(None, "tile", None),
        P("tile", None),
        P(None, "tile", None),
    )
    out_specs = (
        P("nest", "tile", None),
        P("nest", None, "tile", None),
        P("tile", None),
        P(None, "tile", None),
    )
    return jax.shard_map(
        on_device, mesh=mesh, in_specs=in_specs, out_specs=out_specs, check_vma=False
    )
```

time: 23.9 us -> 20.2 us (0.85)
  the two profiles are of different devices: /device:TPU:21 before, /device:TPU:0 now
where the time goes in v1:
time: 20.2 us; the launch traced here: 20.1 us
  Pallas kernels  18.8 us (93%)
  between operations  1.29 us (6%)
    pallas_call x1, Pallas kernels, on_device(): pl.pallas_call(functools.partial(kernel, T, height, breadth, ph, pc), out...  17.9 us
    pallas_call x1, Pallas kernels, on_device(): pl.pallas_call(store, out_shape=[jax.ShapeDtypeStruct(x.shape, f32) for x...  0.88 us

profile of v1, /device:TPU:0, one launch (start us, length us, event | category | flops | bytes accessed | tf_op | source)
XLA Modules:
  0.0 20.1 jit_solution(18129865014124541444)
XLA Ops:
  1.3 17.9 %nested.1 = (f32[1,80,640]{2,1,0:T(8,128)S(1)}, f32[1,2,80,640]{3,2,1,0:T(8,128)S(1)}, f32[16,512]{1,0:T(8,128)S(1)}, f32[2,16,512]{2,1,0:T(8,128)S(1)}) custom-call(f32[1,80,640]{2,1,0:T(8,128)} %fl.1, f32[1,2,80,640]{3,2,1,0:T(8,128)} %ff.1, f32[1,80,640]{2,1,0:T(8,128)} %fd.1, s32[1,80]{1,0:T(1,128)} %shore.1, s32[1,1]{1,0:T(1,128)S(6)} %copy.14.ext, ...), custom_call_target="tpu_custom_call" | custom-call | tf_op jit(solution)/shard_map/nested/pallas_call | solution.py:622
  19.2 0.9 %store.1 = (f32[1,80,640]{2,1,0:T(8,128)}, f32[1,2,80,640]{3,2,1,0:T(8,128)}, f32[16,512]{1,0:T(8,128)}, f32[2,16,512]{2,1,0:T(8,128)}) custom-call(f32[1,80,640]{2,1,0:T(8,128)S(1)} %get-tuple-element.8.refs_0_, f32[1,2,80,640]{3,2,1,0:T(8,128)S(1)} %get-tuple-element.9.refs_1_, f32[16,512]{1,0:T(8,128)S(1)} %get-tuple-element.10.refs_2_, ...), custom_call_target="tpu_custom_call" | custom-call | tf_op jit(solution)/shard_map/store/pallas_call | solution.py:644

commit v2 on v1

--- a/solution.py
+++ b/solution.py
@@ -17,7 +17,7 @@
 RP = 1.0 / (1.0 + DT_COARSE * FRICTION)
 CP = DT_COARSE / DX_COARSE
 FAR = 1.0e6
-WIN = 112
+WIN = 120
 CH = 16
 
 
@@ -72,7 +72,7 @@
     T, height, breadth, ph, pc,
     fl, ff, fd, shore, ext, inter, plev_h, pflux_h, pdep_h, wind_h,
     fl_out, ff_out, pl_out, pf_out,
-    e, q, dep, lim, fxr, cx, fyr, cy, sea0, sead, er, qr, be, bq,
+    e, q, dep, lim, fxr, cx, fyr, cy, cxe, sea0, sead, er, qr, be, bq,
     plv, pfv, pdv, wv, shv, exs, ins, pws, pwb, hs, hr, pks, pkb,
     cs, c0a, c0b, c1, es, e0a, e0b, e1, gs, g0a, g0b, g1,
     ssem, rsem, lsem,
@@ -175,7 +175,38 @@
         for c in group:
             c.arrive()
 
+    for c in locals_[:3]:
+        c.wait()
+    offset = jnp.where(k == 0, ins[0, 0], ins[1, 0])
+    col_a = jnp.where(k == 0, ins[0, 1], ins[1, 1])
+    col_b = jnp.where(k == 0, ins[1, 1], ins[0, 1])
+
+    for c in locals_[3:7]:
+        c.wait()
+    parent = [plv[...], pdv[...], pfv[1], pfv[0], wv[0], wv[1]]
+    block = 0
+    for b in range(1, pc // 128):
+        block = jnp.where(col_a + WIN >= 128 * b, b, block)
+    skip = col_a + WIN - 128 * block
+    lane_p = iota((ph, 128), 1)
+    packed_w = jnp.zeros((ph, 128), jnp.float32)
+    for i, x in enumerate((parent[0], parent[3], parent[2], parent[1], parent[4], parent[5])):
+        cut = [x[:, 128 * b:128 * (b + 1)] for b in range(pc // 128)]
+        here, then = cut[0], cut[1]
+        for b in range(1, pc // 128):
+            here = jnp.where(block == b, cut[b], here)
+            then = jnp.where(block == b, cut[(b + 1) % (pc // 128)], then)
+        by = jnp.where(skip > 16 * i, 128 + 16 * i - skip, 16 * i - skip)
+        both = pltpu.roll(jnp.where(lane_p >= skip, here, then), by, 1)
+        packed_w = jnp.where((lane_p >> 4) == i, both, packed_w)
+    pws[...] = packed_w
     pl.semaphore_wait(barrier, count)
+    windows = [
+        Push(pws.at[0:8, :], pwb.at[3 * ph:3 * ph + 8, :], True, -2, 0),
+        Push(pws.at[:, :], pwb.at[2 * ph:3 * ph, :], True, -1),
+        Push(pws.at[8:ph, :], pwb.at[8:ph, :], True, 1),
+    ]
+    start(windows)
     halo = []
     for d in (1, -1):
         own = slice(height - 8, height) if d == 1 else slice(0, 8)
@@ -188,11 +219,7 @@
         ]
     start(halo)
 
-    for c in locals_[:3]:
-        c.wait()
-    offset = jnp.where(k == 0, ins[0, 0], ins[1, 0])
-    col_a = jnp.where(k == 0, ins[0, 1], ins[1, 1])
-    col_b = jnp.where(k == 0, ins[1, 1], ins[0, 1])
+    pwb[ph:2 * ph, :] = packed_w
 
     diag = iota((height, height), 0) == iota((height, height), 1)
     limit = jnp.sum(jnp.where(diag, shv[...].astype(jnp.float32), 0.0), axis=1, keepdims=True)
@@ -204,29 +231,6 @@
         Push(lim.at[top:top + 8, :], lim.at[halo_s, :], True, -1),
     ]
     start(limits)
-
-    take = hot_of(iota((pc, 128), 0) == col_a + WIN + (iota((pc, 128), 1) & 31))
-    for c in locals_[3:7]:
-        c.wait()
-    parent = [plv[...], pdv[...], pfv[1], pfv[0], wv[0], wv[1]]
-    stack = jnp.concatenate([parent[0], parent[3], parent[2], parent[1], parent[4], parent[5]], axis=0)
-    win = right_hot(stack, take, 3)
-    group = iota((ph, 128), 1) >> 5
-    pack0 = jnp.zeros((ph, 128), jnp.float32)
-    pack1 = jnp.zeros((ph, 128), jnp.float32)
-    for i in range(4):
-        pack0 = jnp.where(group == i, win[i * ph:(i + 1) * ph], pack0)
-    for i in range(2):
-        pack1 = jnp.where(group == i, win[(4 + i) * ph:(5 + i) * ph], pack1)
-    pws[0] = pack0
-    pws[1] = pack1
-    windows = [
-        Push(pws.at[:, 8:ph, :], pwb.at[:, 8:ph, :], True, 1),
-        Push(pws.at[:, :, :], pwb.at[:, 2 * ph:3 * ph, :], True, -1),
-        Push(pws.at[:, 0:8, :], pwb.at[:, 3 * ph:3 * ph + 8, :], True, -2, 0),
-    ]
-    start(windows)
-    pwb[:, ph:2 * ph, :] = pws[...]
 
     pair = iota((8, pc), 0) >> 1
     for at, tile, first in ((0, slice(ph - 8, ph), 2), (1, slice(0, 8), 0)):
@@ -269,8 +273,10 @@
         d0 = dep[sl, :]
         fx = jnp.where(last, 0.0, act * shift_cols(act, -1))
         fxr[sl, :] = fx * RF
-        cx[sl, :] = jnp.where(
-            last, act * jnp.sqrt(d0), (DT_FINE * RF * 0.5) * fx * (d0 + shift_cols(d0, -1)))
+        along = (DT_FINE * RF * 0.5) * fx * (d0 + shift_cols(d0, -1))
+        cx[sl, :] = along
+        cxe[sl, :] = jnp.where(
+            last[:, edge], act[:, edge] * jnp.sqrt(d0[:, edge]), along[:, edge])
         fy = act * act_s
         fyr[sl, :] = fy * RF
         cy[sl, :] = (DT_FINE * RF * 0.5) * fy * (d0 + dep[ss, :])
@@ -278,14 +284,13 @@
     def advance(ef, qf, r0, n, off):
         sl = slice(r0, r0 + n)
         co = slice(r0 + off, r0 + off + n)
-        col = iota((n, breadth), 1)
         e0 = ef[sl, :]
-        east = jnp.where(col == breadth - 1, 0.0, shift_cols(e0, -1))
+        east = shift_cols(e0, -1)
         nx = fxr[co, :] * qf[0, sl, :] - cx[co, :] * (east - e0)
         ny = fyr[co, :] * qf[1, sl, :] - cy[co, :] * (ef[r0 + 1:r0 + n + 1, :] - e0)
         qf[0, sl, :] = nx
         qf[1, sl, :] = ny
-        west = jnp.where(col == 0, 0.0, shift_cols(nx, 1))
+        west = shift_cols(nx, 1)
         north = qf[1, r0 - 1:r0 + n - 1, :]
         ef[sl, :] = e0 - DT_FINE * (nx - west + ny - north)
 
@@ -314,13 +319,11 @@
     lev_at = 128 - WIN
     flux_at = 127 - WIN
     rowsum = hot_of(iota((32, height), 0) == offset + fdiv5(iota((32, height), 1)))
-    l32 = iota((128, 128), 1) & 31
-    sum_same = hot_of(fdiv5(iota((128, 128), 0) + (breadth - 128)) == WIN + l32)
     begin = 0
     for s in range(128, breadth - 255, 128):
         begin = jnp.where(RATIO * (col_b - col_a + 127) >= s, s, begin)
     sum_other = hot_of(
-        fdiv5(iota((256, 128), 0) + begin) == col_b - col_a + WIN + (iota((256, 128), 1) & 31))
+        fdiv5(iota((256, 128), 0) + begin) == col_b - col_a + WIN + (iota((256, 128), 1) & 15))
     spread = hot_of(
         iota((rows - 16, 4 * ph), 1)
         == ph + offset + fdiv5(iota((rows - 16, 4 * ph), 0) + 32) - 8
@@ -342,10 +345,8 @@
     coefficients(8)
     coefficients(rows - 8 - CH)
 
-    b0 = pwb[0]
-    b1 = pwb[1]
-    we, wux, wuy, wd = b0, shift_cols(b0, -32), shift_cols(b0, -64), shift_cols(b0, -96)
-    wwx, wwy = b1, shift_cols(b1, -32)
+    we = pwb[...]
+    wux, wuy, wd, wwx, wwy = [shift_cols(we, -16 * i) for i in range(1, 6)]
     whx = 0.5 * (wd + shift_cols(wd, -1))
     why = 0.5 * (wd + shift_rows(wd, -1))
 
@@ -361,7 +362,7 @@
         z = jnp.where(lane == 124, shift_cols(nux, 124 - flux_at), z)
         s = left_hot(spread, z, 3)
         act = jnp.where(float(breadth - 1) >= lim[inner, :], 1.0, 0.0)
-        cel = cx[inner, breadth - 128:]
+        cel = cxe[inner, :]
         old = act * shift_cols(s, 1) - cel * s
         new = act * shift_cols(s, 3) - cel * shift_cols(s, 2)
         keep = lane_f == 127
@@ -374,7 +375,7 @@
             e0 = er[inner, :]
             east = jnp.where(lane_f == 127, 0.0, shift_cols(e0, -1))
             sea = sea0[inner, :] + w * sead[inner, :]
-            nx = fxr[inner, edge] * qr[0, inner, :] - cx[inner, edge] * (east - e0) + sea
+            nx = fxr[inner, edge] * qr[0, inner, :] - cxe[inner, :] * (east - e0) + sea
             ny = fyr[inner, edge] * qr[1, inner, :] - cy[inner, edge] * (er[9:rows - 7, :] - e0)
             qr[0, inner, :] = nx
             qr[1, inner, :] = ny
@@ -404,7 +405,7 @@
     edge_columns()
     merge_edge(inner)
 
-    glane = iota((32, 128), 1) >> 5
+    glane = iota((32, 128), 1) >> 4
 
     def packed(res, n):
         out = res[0:32]
@@ -426,7 +427,22 @@
             part = [mm(rowsum, act.astype(jnp.bfloat16))] + part
         return right_hot(jnp.concatenate(part, axis=0), columns, 2)
 
-    pks[0] = packed(restrict(wet(128, breadth - 128), er[mid, :], qr[0, mid, :], qr[1, mid, :], sum_same, True), 4)
+
+    def last_sums(with_count, first, step):
+        act = wet(128, breadth - 128)
+        parts = [act * er[mid, :], qr[0, mid, :], qr[1, mid, :]]
+        if with_count:
+            parts = [act] + parts
+        lane_m = iota((height, 128), 1)
+        out = jnp.zeros((height, 128), jnp.float32)
+        for i, x in enumerate(parts):
+            y = x + shift_cols(x, 1)
+            y = y + shift_cols(y, 2) + shift_cols(x, 4)
+            at = first + step * i
+            out = jnp.where(lane_m == at, shift_cols(y, at + 1), out)
+        return left_hot(rowsum, out, 2)
+
+    pks[0] = last_sums(True, 127 - WIN, 16)
 
     def there(ref):
         out = ref[mid, 0:256]
@@ -507,15 +523,14 @@
         pkb[4][0:ph] + nxt[ph:2 * ph],
     ], axis=0) * (1.0 / (RATIO * RATIO))
     keep = 1.0 - sums
-    u1e = n1e * keep + shift_cols(sums, -32)
-    u1x = n1x * keep + shift_cols(sums, -64)
-    u1y = n1y * keep + shift_cols(sums, -96)
+    u1e = n1e * keep + shift_cols(sums, -16)
+    u1x = n1x * keep + shift_cols(sums, -32)
+    u1y = n1y * keep + shift_cols(sums, -48)
     n2e, n2x, _ = window_step(u1e, u1x, u1y)
     set_sea(u1e, u1x, n2e, n2x)
     edge_columns()
 
-    sum_last = hot_of(iota((128, 128), 0) >= 128 - RATIO)
-    gs[...] = packed(restrict(wet(128, breadth - 128), er[mid, :], qr[0, mid, :], qr[1, mid, :], sum_last, False), 3)
+    gs[...] = last_sums(False, 0, 1)
     sums3 = final_sums(gs, g0a, g0b, g1, lambda i: (slice(ph * i, ph * (i + 1)), slice(None)))
 
     merge_edge(mid)
@@ -586,8 +601,8 @@
     z1 = g1[...] * (1.0 / (RATIO * RATIO))
     outs = []
     for i in range(3):
-        v0 = jnp.broadcast_to(z0[:, 32 * i:32 * i + 1], (ph, pc))
-        v1 = jnp.broadcast_to(z1[:, 32 * i:32 * i + 1], (ph, pc))
+        v0 = jnp.broadcast_to(z0[:, i:i + 1], (ph, pc))
+        v1 = jnp.broadcast_to(z1[:, i:i + 1], (ph, pc))
         outs.append(base[i] + jnp.where(at_0, v0, 0.0) + jnp.where(at_1, v1, 0.0))
     pl_out[...] = outs[0]
     pf_out[0] = outs[1]
@@ -626,11 +641,11 @@
         out_specs=[vm] * 4,
         scratch_shapes=[
             fine, vmem(2, rows, breadth), fine, strip,
-            fine, fine, fine, fine, strip, strip, strip, vmem(2, rows, 128),
+            fine, fine, fine, fine, strip, strip, strip, strip, vmem(2, rows, 128),
             vmem(2, 40, breadth), vmem(2, 2, 40, breadth),
             vmem(ph, pc), vmem(2, ph, pc), vmem(ph, pc), vmem(2, ph, pc),
             pltpu.VMEM((1, height), jnp.int32), pltpu.SMEM((1, 1), jnp.int32), pltpu.SMEM((2, 2), jnp.int32),
-            vmem(2, ph, 128), vmem(2, 4 * ph, 128), vmem(2, 16, pc), vmem(2, 16, pc),
+            vmem(ph, 128), vmem(4 * ph, 128), vmem(2, 16, pc), vmem(2, 16, pc),
             vmem(2, 2 * ph, 128), vmem(7, 2 * ph, 128),
             vmem(4, 2 * ph, 128), vmem(4, 2 * ph, 128), vmem(4, 2 * ph, 128), vmem(4, 2 * ph, 128),
             vmem(3, 2 * ph, 128), vmem(3, ph, 128), vmem(3, ph, 128), vmem(3, ph, 128),

time: 20.2 us -> 18.8 us (0.931)
  Pallas kernels: 18.8 us -> 17.4 us
    pallas_call x1, Pallas kernels: 17.9 us -> 16.5 us  [on_device(): pl.pallas_call(functools.partial(kernel, T, height, breadth, ph, pc), out...]
where the time goes in v2:
time: 18.8 us; the launch traced here: 18.7 us
  Pallas kernels  17.4 us (93%)
  between operations  1.29 us (7%)
    pallas_call x1, Pallas kernels, on_device(): pl.pallas_call(functools.partial(kernel, T, height, breadth, ph, pc), out...  16.5 us
    pallas_call x1, Pallas kernels, on_device(): pl.pallas_call(store, out_shape=[jax.ShapeDtypeStruct(x.shape, f32) for x...  0.88 us

profile of v2, /device:TPU:0, one launch (start us, length us, event | category | flops | bytes accessed | tf_op | source)
XLA Modules:
  0.0 18.7 jit_solution(15685721650340503574)
XLA Ops:
  1.3 16.5 %nested.1 = (f32[1,80,640]{2,1,0:T(8,128)S(1)}, f32[1,2,80,640]{3,2,1,0:T(8,128)S(1)}, f32[16,512]{1,0:T(8,128)S(1)}, f32[2,16,512]{2,1,0:T(8,128)S(1)}) custom-call(f32[1,80,640]{2,1,0:T(8,128)} %fl.1, f32[1,2,80,640]{3,2,1,0:T(8,128)} %ff.1, f32[1,80,640]{2,1,0:T(8,128)} %fd.1, s32[1,80]{1,0:T(1,128)} %shore.1, s32[1,1]{1,0:T(1,128)S(6)} %copy.14.ext, ...), custom_call_target="tpu_custom_call" | custom-call | tf_op jit(solution)/shard_map/nested/pallas_call | solution.py:637
  17.8 0.9 %store.1 = (f32[1,80,640]{2,1,0:T(8,128)}, f32[1,2,80,640]{3,2,1,0:T(8,128)}, f32[16,512]{1,0:T(8,128)}, f32[2,16,512]{2,1,0:T(8,128)}) custom-call(f32[1,80,640]{2,1,0:T(8,128)S(1)} %get-tuple-element.8.refs_0_, f32[1,2,80,640]{3,2,1,0:T(8,128)S(1)} %get-tuple-element.9.refs_1_, f32[16,512]{1,0:T(8,128)S(1)} %get-tuple-element.10.refs_2_, ...), custom_call_target="tpu_custom_call" | custom-call | tf_op jit(solution)/shard_map/store/pallas_call | solution.py:659

commit v3 on v2

--- a/solution.py
+++ b/solution.py
@@ -281,18 +281,27 @@
         fyr[sl, :] = fy * RF
         cy[sl, :] = (DT_FINE * RF * 0.5) * fy * (d0 + dep[ss, :])
 
-    def advance(ef, qf, r0, n, off):
-        sl = slice(r0, r0 + n)
-        co = slice(r0 + off, r0 + off + n)
-        e0 = ef[sl, :]
-        east = shift_cols(e0, -1)
-        nx = fxr[co, :] * qf[0, sl, :] - cx[co, :] * (east - e0)
-        ny = fyr[co, :] * qf[1, sl, :] - cy[co, :] * (ef[r0 + 1:r0 + n + 1, :] - e0)
-        qf[0, sl, :] = nx
-        qf[1, sl, :] = ny
-        west = shift_cols(nx, 1)
-        north = qf[1, r0 - 1:r0 + n - 1, :]
-        ef[sl, :] = e0 - DT_FINE * (nx - west + ny - north)
+    r8 = iota((8, breadth), 0)
+
+    def advance(ef, qf, first, past, off):
+        after = ef[first:first + 8, :]
+        after_up = shift_rows(after, -1)
+        before_down = shift_rows(qf[1, first - 8:first, :], 1)
+        for r0 in range(first, past, 8):
+            sl = slice(r0, r0 + 8)
+            co = slice(r0 + off, r0 + off + 8)
+            e0, e0_up = after, after_up
+            after = ef[r0 + 8:r0 + 16, :]
+            after_up = shift_rows(after, -1)
+            south = jnp.where(r8 == 7, after_up, e0_up)
+            nx = fxr[co, :] * qf[0, sl, :] - cx[co, :] * (shift_cols(e0, -1) - e0)
+            ny = fyr[co, :] * qf[1, sl, :] - cy[co, :] * (south - e0)
+            qf[0, sl, :] = nx
+            qf[1, sl, :] = ny
+            down = shift_rows(ny, 1)
+            north = jnp.where(r8 == 0, before_down, down)
+            before_down = down
+            ef[sl, :] = e0 - DT_FINE * (nx - shift_cols(nx, 1) + ny - north)
 
     locals_[7].wait()
     for r0 in range(8 + CH, rows - 8 - CH, CH):
@@ -308,16 +317,13 @@
         qr[i, mid, :] = q[i, mid, edge]
 
     def inside(step, carry):
-        for r0 in range(8 + CH, rows - 8 - CH, CH):
-            advance(e, q, r0, CH, 0)
+        advance(e, q, 8 + CH, rows - 8 - CH, 0)
         return carry
 
     lax.fori_loop(0, SUBSTEPS, inside, 0)
 
-    lane = iota((4 * ph, 128), 1)
     lane_f = iota((rows - 16, 128), 1)
-    lev_at = 128 - WIN
-    flux_at = 127 - WIN
+    level_at = 128 - WIN
     rowsum = hot_of(iota((32, height), 0) == offset + fdiv5(iota((32, height), 1)))
     begin = 0
     for s in range(128, breadth - 255, 128):
@@ -329,7 +335,8 @@
         == ph + offset + fdiv5(iota((rows - 16, 4 * ph), 0) + 32) - 8
     )
     wrow = (t - 1) * ph + iota((4 * ph, 128), 0)
-    wcol = col_a + WIN + iota((4 * ph, 128), 1)
+    wlane = iota((4 * ph, 128), 1)
+    wcol = col_a + 1 + jnp.where(wlane < 64, wlane + 128, wlane)
     w_row_open = jnp.where((wrow >= 0) & (wrow < ph * T - 1), 1.0, 0.0)
     w_col_open = jnp.where(wcol < pc - 1, 1.0, 0.0)
 
@@ -345,42 +352,49 @@
     coefficients(8)
     coefficients(rows - 8 - CH)
 
-    we = pwb[...]
-    wux, wuy, wd, wwx, wwy = [shift_cols(we, -16 * i) for i in range(1, 6)]
-    whx = 0.5 * (wd + shift_cols(wd, -1))
+    pw = pwb[...]
+    here = lambda x, i: shift_cols(x, 127 - level_at - 16 * i)
+    west_of = lambda x, i: shift_cols(x, 128 - level_at - 16 * i)
+    we, wux, wuy, wd, wwx, wwy = [here(pw, i) for i in range(6)]
+    wuxw, wdw, wwxw = [west_of(pw, i) for i in (1, 3, 4)]
+    whx = 0.5 * (wd + shift_cols(pw, 126 - level_at - 48))
+    whxw = 0.5 * (wdw + wd)
     why = 0.5 * (wd + shift_rows(wd, -1))
 
-    def window_step(we, wux, wuy):
-        nx, ny = parent_step(we, wux, wuy, whx, why, wwx, wwy, w_col_open, w_row_open)
-        ne = we - CP * (nx - shift_cols(nx, 1) + ny - shift_rows(ny, 1))
-        return ne, nx, ny
+    def window_step(we, wux, wuxw, wuy):
+        nx = w_col_open * (wux - CP * whx * (shift_cols(we, -1) - we) + DT_COARSE * wwx) * RP
+        nxw = (wuxw - CP * whxw * (we - shift_cols(we, 1)) + DT_COARSE * wwxw) * RP
+        ny = w_row_open * (wuy - CP * why * (shift_rows(we, -1) - we) + DT_COARSE * wwy) * RP
+        ne = we - CP * (nx - nxw + ny - shift_rows(ny, 1))
+        return ne, nx, nxw, ny
 
     def set_sea(oe, oux, ne, nux):
-        z = jnp.where(lane == 127, shift_cols(oe, 127 - lev_at), 0.0)
-        z = jnp.where(lane == 126, shift_cols(oux, 126 - flux_at), z)
-        z = jnp.where(lane == 125, shift_cols(ne, 125 - lev_at), z)
-        z = jnp.where(lane == 124, shift_cols(nux, 124 - flux_at), z)
-        s = left_hot(spread, z, 3)
+        s = left_hot(spread, jnp.concatenate([oe, oux, ne, nux], axis=1), 3)
+        ea, qb, ea_new, qb_new = [s[:, 128 * i:128 * (i + 1)] for i in range(4)]
         act = jnp.where(float(breadth - 1) >= lim[inner, :], 1.0, 0.0)
         cel = cxe[inner, :]
-        old = act * shift_cols(s, 1) - cel * s
-        new = act * shift_cols(s, 3) - cel * shift_cols(s, 2)
+        old = act * qb - cel * ea
+        new = act * qb_new - cel * ea_new
         keep = lane_f == 127
         sea0[inner, :] = jnp.where(keep, old, 0.0)
         sead[inner, :] = jnp.where(keep, new - old, 0.0)
 
     def edge_columns():
+        e0, qx, qy = er[inner, :], qr[0, inner, :], qr[1, inner, :]
+        sea, more = sea0[inner, :], sead[inner, :]
+        kx, ky = cxe[inner, :], cy[inner, edge]
+        fx, fy = fxr[inner, edge], fyr[inner, edge]
+        qxw, kxw, fxw = shift_cols(qx, 1), shift_cols(kx, 1), shift_cols(fx, 1)
         for n in range(SUBSTEPS):
             w = (n + 0.5) / SUBSTEPS
-            e0 = er[inner, :]
             east = jnp.where(lane_f == 127, 0.0, shift_cols(e0, -1))
-            sea = sea0[inner, :] + w * sead[inner, :]
-            nx = fxr[inner, edge] * qr[0, inner, :] - cxe[inner, :] * (east - e0) + sea
-            ny = fyr[inner, edge] * qr[1, inner, :] - cy[inner, edge] * (er[9:rows - 7, :] - e0)
-            qr[0, inner, :] = nx
-            qr[1, inner, :] = ny
-            north = qr[1, 7:rows - 9, :]
-            er[inner, :] = e0 - DT_FINE * (nx - shift_cols(nx, 1) + ny - north)
+            qx = fx * qx - kx * (east - e0) + (sea + w * more)
+            qxw = fxw * qxw - kxw * (e0 - shift_cols(e0, 1))
+            qy = fy * qy - ky * (shift_rows(e0, -1) - e0)
+            e0 = e0 - DT_FINE * (qx - qxw + qy - shift_rows(qy, 1))
+        er[inner, :] = e0
+        qr[0, inner, :] = qx
+        qr[1, inner, :] = qy
 
     def merge_edge(where):
         n = where.stop - where.start
@@ -390,18 +404,16 @@
             q[i, where, edge] = jnp.where(keep, qr[i, where, :], q[i, where, edge])
 
     for n in range(SUBSTEPS):
-        for r0 in (8, 16, 24):
-            advance(be.at[0], bq.at[0], r0, 8, 0)
-            advance(be.at[1], bq.at[1], r0, 8, rows - 40)
-    r8 = iota((8, breadth), 0)
+        advance(be.at[0], bq.at[0], 8, 32, 0)
+        advance(be.at[1], bq.at[1], 8, 32, rows - 40)
     for dst, bnd in ((e, lambda b: be.at[b]), (q.at[0], lambda b: bq.at[b, 0]), (q.at[1], lambda b: bq.at[b, 1])):
         dst[8:24, :] = bnd(0)[8:24, :]
         dst[24:32, :] = jnp.where(r8 < 4, bnd(0)[24:32, :], dst[24:32, :])
         dst[rows - 32:rows - 24, :] = jnp.where(r8 >= 4, bnd(1)[8:16, :], dst[rows - 32:rows - 24, :])
         dst[rows - 24:rows - 8, :] = bnd(1)[16:32, :]
 
-    n1e, n1x, n1y = window_step(we, wux, wuy)
-    set_sea(we, wux, n1e, n1x)
+    n1e, n1x, n1xw, n1y = window_step(we, wux, wuxw, wuy)
+    set_sea(we, wuxw, n1e, n1xw)
     edge_columns()
     merge_edge(inner)
 
@@ -428,21 +440,21 @@
         return right_hot(jnp.concatenate(part, axis=0), columns, 2)
 
 
-    def last_sums(with_count, first, step):
+    lane_m = iota((height, 128), 1)
+
+    def last_sums(with_count):
         act = wet(128, breadth - 128)
         parts = [act * er[mid, :], qr[0, mid, :], qr[1, mid, :]]
         if with_count:
             parts = [act] + parts
-        lane_m = iota((height, 128), 1)
-        out = jnp.zeros((height, 128), jnp.float32)
-        for i, x in enumerate(parts):
-            y = x + shift_cols(x, 1)
-            y = y + shift_cols(y, 2) + shift_cols(x, 4)
-            at = first + step * i
-            out = jnp.where(lane_m == at, shift_cols(y, at + 1), out)
+        x = 0.0
+        for i, part in enumerate(parts):
+            x = jnp.where((lane_m >> 4) == i, shift_cols(part, 16 * i + level_at), x)
+        y = x + ((shift_cols(x, 1) + shift_cols(x, 2)) + (shift_cols(x, 3) + shift_cols(x, 4)))
+        out = jnp.where((lane_m & 15) == 127 - WIN, y, 0.0)
         return left_hot(rowsum, out, 2)
 
-    pks[0] = last_sums(True, 127 - WIN, 16)
+    pks[0] = last_sums(True)
 
     def there(ref):
         out = ref[mid, 0:256]
@@ -481,8 +493,7 @@
     qr[...] = q[:, :, edge]
 
     def everywhere(step, carry):
-        for r0 in range(8, rows - 8, CH):
-            advance(e, q, r0, CH, 0)
+        advance(e, q, 8, rows - 8, 0)
         return carry
 
     lax.fori_loop(0, SUBSTEPS, everywhere, 0)
@@ -522,15 +533,16 @@
         nxt[0:ph] + beside[ph:2 * ph],
         pkb[4][0:ph] + nxt[ph:2 * ph],
     ], axis=0) * (1.0 / (RATIO * RATIO))
-    keep = 1.0 - sums
-    u1e = n1e * keep + shift_cols(sums, -16)
-    u1x = n1x * keep + shift_cols(sums, -32)
-    u1y = n1y * keep + shift_cols(sums, -48)
-    n2e, n2x, _ = window_step(u1e, u1x, u1y)
-    set_sea(u1e, u1x, n2e, n2x)
+    keep = 1.0 - here(sums, 0)
+    u1e = n1e * keep + here(sums, 1)
+    u1x = n1x * keep + here(sums, 2)
+    u1xw = n1xw * (1.0 - west_of(sums, 0)) + west_of(sums, 2)
+    u1y = n1y * keep + here(sums, 3)
+    n2e, _, n2xw, _ = window_step(u1e, u1x, u1xw, u1y)
+    set_sea(u1e, u1xw, n2e, n2xw)
     edge_columns()
 
-    gs[...] = last_sums(False, 0, 1)
+    gs[...] = last_sums(False)
     sums3 = final_sums(gs, g0a, g0b, g1, lambda i: (slice(ph * i, ph * (i + 1)), slice(None)))
 
     merge_edge(mid)
@@ -601,8 +613,8 @@
     z1 = g1[...] * (1.0 / (RATIO * RATIO))
     outs = []
     for i in range(3):
-        v0 = jnp.broadcast_to(z0[:, i:i + 1], (ph, pc))
-        v1 = jnp.broadcast_to(z1[:, i:i + 1], (ph, pc))
+        v0 = jnp.broadcast_to(z0[:, 127 - WIN + 16 * i:128 - WIN + 16 * i], (ph, pc))
+        v1 = jnp.broadcast_to(z1[:, 127 - WIN + 16 * i:128 - WIN + 16 * i], (ph, pc))
         outs.append(base[i] + jnp.where(at_0, v0, 0.0) + jnp.where(at_1, v1, 0.0))
     pl_out[...] = outs[0]
     pf_out[0] = outs[1]

time: 18.8 us -> 18 us (0.957)
  Pallas kernels: 17.4 us -> 16.6 us
    pallas_call x1, Pallas kernels: 16.5 us -> 15.7 us  [on_device(): pl.pallas_call(functools.partial(kernel, T, height, breadth, ph, pc), out...]
where the time goes in v3:
time: 18 us; the launch traced here: 17.8 us
  Pallas kernels  16.6 us (92%)
  between operations  1.29 us (7%)
    pallas_call x1, Pallas kernels, on_device(): pl.pallas_call(functools.partial(kernel, T, height, breadth, ph, pc), out...  15.7 us
    pallas_call x1, Pallas kernels, on_device(): pl.pallas_call(store, out_shape=[jax.ShapeDtypeStruct(x.shape, f32) for x...  0.88 us

profile of v3, /device:TPU:0, one launch (start us, length us, event | category | flops | bytes accessed | tf_op | source)
XLA Modules:
  0.0 17.8 jit_solution(15644303459411961825)
XLA Ops:
  1.3 15.7 %nested.1 = (f32[1,80,640]{2,1,0:T(8,128)S(1)}, f32[1,2,80,640]{3,2,1,0:T(8,128)S(1)}, f32[16,512]{1,0:T(8,128)S(1)}, f32[2,16,512]{2,1,0:T(8,128)S(1)}) custom-call(f32[1,80,640]{2,1,0:T(8,128)} %fl.1, f32[1,2,80,640]{3,2,1,0:T(8,128)} %ff.1, f32[1,80,640]{2,1,0:T(8,128)} %fd.1, s32[1,80]{1,0:T(1,128)} %shore.1, s32[1,1]{1,0:T(1,128)S(6)} %copy.14.ext, ...), custom_call_target="tpu_custom_call" | custom-call | tf_op jit(solution)/shard_map/nested/pallas_call | solution.py:649
  17.0 0.9 %store.1 = (f32[1,80,640]{2,1,0:T(8,128)}, f32[1,2,80,640]{3,2,1,0:T(8,128)}, f32[16,512]{1,0:T(8,128)}, f32[2,16,512]{2,1,0:T(8,128)}) custom-call(f32[1,80,640]{2,1,0:T(8,128)S(1)} %get-tuple-element.8.refs_0_, f32[1,2,80,640]{3,2,1,0:T(8,128)S(1)} %get-tuple-element.9.refs_1_, f32[16,512]{1,0:T(8,128)S(1)} %get-tuple-element.10.refs_2_, ...), custom_call_target="tpu_custom_call" | custom-call | tf_op jit(solution)/shard_map/store/pallas_call | solution.py:671

commit v4 on v3

--- a/solution.py
+++ b/solution.py
@@ -38,6 +38,10 @@
     return sum(mm(hot, p) for p in parts_of(x, n))
 
 
+def stacked_hot(hot, x, n):
+    return mm(hot, jnp.concatenate(parts_of(x, n), axis=0))
+
+
 def right_hot(x, hot, n):
     return sum(mm(p, hot) for p in parts_of(x, n))
 
@@ -75,7 +79,7 @@
     e, q, dep, lim, fxr, cx, fyr, cy, cxe, sea0, sead, er, qr, be, bq,
     plv, pfv, pdv, wv, shv, exs, ins, pws, pwb, hs, hr, pks, pkb,
     cs, c0a, c0b, c1, es, e0a, e0b, e1, gs, g0a, g0b, g1,
-    ssem, rsem, lsem,
+    ssem, rsem, lsem, ready,
 ):
     k = lax.axis_index("nest")
     t = lax.axis_index("tile")
@@ -135,13 +139,9 @@
     for d in (1, -1):
         greet(k, d)
     greet(ko, 0)
-    greet(ko, -1)
     greet(k, 2, 0)
-    greet(ko, 1, 0)
-    greet(ko, 2, 0)
-    greet(ko, -2, 1)
-    count = (expect(1) + expect(-1) + 1 + expect(1) + expect(-2, 0) + expect(2, 0)
-             + expect(-1, 1) + expect(-2, 1))
+    greet(k, -2, 1)
+    count = expect(1) + expect(-1) + 1 + expect(-2, 0) + expect(2, 1)
 
     pushes = []
 
@@ -201,6 +201,7 @@
         packed_w = jnp.where((lane_p >> 4) == i, both, packed_w)
     pws[...] = packed_w
     pl.semaphore_wait(barrier, count)
+    pl.semaphore_signal(ready, inc=1, device_id=(ko, t), device_id_type=pl.DeviceIdType.MESH)
     windows = [
         Push(pws.at[0:8, :], pwb.at[3 * ph:3 * ph + 8, :], True, -2, 0),
         Push(pws.at[:, :], pwb.at[2 * ph:3 * ph, :], True, -1),
@@ -243,7 +244,6 @@
         Push(hs.at[0], hr.at[0], True, 1),
         Push(hs.at[1], hr.at[1], True, -1),
     ]
-    start(parent_halo)
 
     for s in (slice(0, 8), slice(rows - 8, rows)):
         e[s, :] = zrow
@@ -331,35 +331,16 @@
     sum_other = hot_of(
         fdiv5(iota((256, 128), 0) + begin) == col_b - col_a + WIN + (iota((256, 128), 1) & 15))
     spread = hot_of(
-        iota((rows - 16, 4 * ph), 1)
-        == ph + offset + fdiv5(iota((rows - 16, 4 * ph), 0) + 32) - 8
+        iota((rows - 16, 8 * ph), 1) % (4 * ph)
+        == ph + offset + fdiv5(iota((rows - 16, 8 * ph), 0) + 32) - 8
     )
+    twice = iota((32, 2 * height), 1)
+    rowsum2 = hot_of(iota((32, 2 * height), 0) == offset + fdiv5(jnp.where(twice >= height, twice - height, twice)))
     wrow = (t - 1) * ph + iota((4 * ph, 128), 0)
     wlane = iota((4 * ph, 128), 1)
     wcol = col_a + 1 + jnp.where(wlane < 64, wlane + 128, wlane)
     w_row_open = jnp.where((wrow >= 0) & (wrow < ph * T - 1), 1.0, 0.0)
     w_col_open = jnp.where(wcol < pc - 1, 1.0, 0.0)
-
-    arrive(halo)
-    arrive(limits)
-    arrive(windows)
-
-    er[halo_n, :] = be[0, 8:16, edge]
-    er[halo_s, :] = be[1, 24:32, edge]
-    for i in range(2):
-        qr[i, halo_n, :] = bq[0, i, 8:16, edge]
-        qr[i, halo_s, :] = bq[1, i, 24:32, edge]
-    coefficients(8)
-    coefficients(rows - 8 - CH)
-
-    pw = pwb[...]
-    here = lambda x, i: shift_cols(x, 127 - level_at - 16 * i)
-    west_of = lambda x, i: shift_cols(x, 128 - level_at - 16 * i)
-    we, wux, wuy, wd, wwx, wwy = [here(pw, i) for i in range(6)]
-    wuxw, wdw, wwxw = [west_of(pw, i) for i in (1, 3, 4)]
-    whx = 0.5 * (wd + shift_cols(pw, 126 - level_at - 48))
-    whxw = 0.5 * (wdw + wd)
-    why = 0.5 * (wd + shift_rows(wd, -1))
 
     def window_step(we, wux, wuxw, wuy):
         nx = w_col_open * (wux - CP * whx * (shift_cols(we, -1) - we) + DT_COARSE * wwx) * RP
@@ -368,8 +349,10 @@
         ne = we - CP * (nx - nxw + ny - shift_rows(ny, 1))
         return ne, nx, nxw, ny
 
-    def set_sea(oe, oux, ne, nux):
-        s = left_hot(spread, jnp.concatenate([oe, oux, ne, nux], axis=1), 3)
+    def spread_sea(oe, oux, ne, nux):
+        return stacked_hot(spread, jnp.concatenate([oe, oux, ne, nux], axis=1), 2)
+
+    def set_sea(s):
         ea, qb, ea_new, qb_new = [s[:, 128 * i:128 * (i + 1)] for i in range(4)]
         act = jnp.where(float(breadth - 1) >= lim[inner, :], 1.0, 0.0)
         cel = cxe[inner, :]
@@ -403,6 +386,28 @@
         for i in range(2):
             q[i, where, edge] = jnp.where(keep, qr[i, where, :], q[i, where, edge])
 
+    arrive(halo)
+    arrive(limits)
+    er[halo_n, :] = be[0, 8:16, edge]
+    er[halo_s, :] = be[1, 24:32, edge]
+    for i in range(2):
+        qr[i, halo_n, :] = bq[0, i, 8:16, edge]
+        qr[i, halo_s, :] = bq[1, i, 24:32, edge]
+    coefficients(8)
+    coefficients(rows - 8 - CH)
+
+    arrive(windows)
+    pw = pwb[...]
+    here = lambda x, i: shift_cols(x, 127 - level_at - 16 * i)
+    west_of = lambda x, i: shift_cols(x, 128 - level_at - 16 * i)
+    we, wux, wuy, wd, wwx, wwy = [here(pw, i) for i in range(6)]
+    wuxw, wdw, wwxw = [west_of(pw, i) for i in (1, 3, 4)]
+    whx = 0.5 * (wd + shift_cols(pw, 126 - level_at - 48))
+    whxw = 0.5 * (wdw + wd)
+    why = 0.5 * (wd + shift_rows(wd, -1))
+
+    n1e, n1x, n1xw, n1y = window_step(we, wux, wuxw, wuy)
+    sea = spread_sea(we, wuxw, n1e, n1xw)
     for n in range(SUBSTEPS):
         advance(be.at[0], bq.at[0], 8, 32, 0)
         advance(be.at[1], bq.at[1], 8, 32, rows - 40)
@@ -412,8 +417,7 @@
         dst[rows - 32:rows - 24, :] = jnp.where(r8 >= 4, bnd(1)[8:16, :], dst[rows - 32:rows - 24, :])
         dst[rows - 24:rows - 8, :] = bnd(1)[16:32, :]
 
-    n1e, n1x, n1xw, n1y = window_step(we, wux, wuxw, wuy)
-    set_sea(we, wuxw, n1e, n1xw)
+    set_sea(sea)
     edge_columns()
     merge_edge(inner)
 
@@ -452,7 +456,7 @@
             x = jnp.where((lane_m >> 4) == i, shift_cols(part, 16 * i + level_at), x)
         y = x + ((shift_cols(x, 1) + shift_cols(x, 2)) + (shift_cols(x, 3) + shift_cols(x, 4)))
         out = jnp.where((lane_m & 15) == 127 - WIN, y, 0.0)
-        return left_hot(rowsum, out, 2)
+        return stacked_hot(rowsum2, out, 2)
 
     pks[0] = last_sums(True)
 
@@ -463,6 +467,7 @@
         return out
 
     pks[1] = packed(restrict(wet(256, begin), there(e), there(q.at[0]), there(q.at[1]), sum_other, True), 4)
+    pl.semaphore_wait(ready, 1)
     near = start([
         Push(pks.at[1], pkb.at[0], False, 0),
         Push(pks.at[1, 8:32, :], pkb.at[1, 8:32, :], False, 1),
@@ -473,6 +478,7 @@
         Push(pks.at[0, 0:24, :], pkb.at[6, 0:24, :], True, -1),
     ])
 
+    start(parent_halo)
     colsum = hot_of(fdiv5(iota((breadth, 128), 0)) == iota((breadth, 128), 1))
     s1 = restrict(wet(breadth, 0), e[mid, :], q[0, mid, :], q[1, mid, :], colsum, True)
     for i in range(4):
@@ -539,7 +545,7 @@
     u1xw = n1xw * (1.0 - west_of(sums, 0)) + west_of(sums, 2)
     u1y = n1y * keep + here(sums, 3)
     n2e, _, n2xw, _ = window_step(u1e, u1x, u1xw, u1y)
-    set_sea(u1e, u1xw, n2e, n2xw)
+    set_sea(spread_sea(u1e, u1xw, n2e, n2xw))
     edge_columns()
 
     gs[...] = last_sums(False)
@@ -608,6 +614,9 @@
     base = [t2[i][own_p] * held + g[i] for i in range(3)]
     at_0 = gcol[own_p] == col_0 + (breadth // RATIO - 1)
     at_1 = gcol[own_p] == col_1 + (breadth // RATIO - 1)
+    for c in pushes:
+        if c not in sums3:
+            c.sent()
     arrive(sums3)
     z0 = (g0a[...] + g0b[...]) * (1.0 / (RATIO * RATIO))
     z1 = g1[...] * (1.0 / (RATIO * RATIO))
@@ -619,7 +628,7 @@
     pl_out[...] = outs[0]
     pf_out[0] = outs[1]
     pf_out[1] = outs[2]
-    for c in pushes:
+    for c in sums3:
         c.sent()
 
 
@@ -662,7 +671,7 @@
             vmem(4, 2 * ph, 128), vmem(4, 2 * ph, 128), vmem(4, 2 * ph, 128), vmem(4, 2 * ph, 128),
             vmem(3, 2 * ph, 128), vmem(3, ph, 128), vmem(3, ph, 128), vmem(3, ph, 128),
             vmem(2 * ph, 128), vmem(ph, 128), vmem(ph, 128), vmem(ph, 128),
-            dma((36,)), dma((36,)), dma((10,)),
+            dma((36,)), dma((36,)), dma((10,)), pltpu.SemaphoreType.REGULAR,
         ],
         compiler_params=pltpu.CompilerParams(
             collective_id=0, has_side_effects=True, vmem_limit_bytes=48 * 1024 * 1024),

time: 18 us -> 17.4 us (0.967)
  the two profiles are of different devices: /device:TPU:0 before, /device:TPU:7 now
where the time goes in v4:
time: 17.4 us; the launch traced here: 17.2 us
  Pallas kernels  16 us (92%)
  between operations  1.29 us (7%)
    pallas_call x1, Pallas kernels, on_device(): pl.pallas_call(functools.partial(kernel, T, height, breadth, ph, pc), out...  15.1 us
    pallas_call x1, Pallas kernels, on_device(): pl.pallas_call(store, out_shape=[jax.ShapeDtypeStruct(x.shape, f32) for x...  0.88 us

profile of v4, /device:TPU:7, one launch (start us, length us, event | category | flops | bytes accessed | tf_op | source)
XLA Modules:
  0.0 17.2 jit_solution(9057478188733965749)
XLA Ops:
  1.3 15.1 %nested.1 = (f32[1,80,640]{2,1,0:T(8,128)S(1)}, f32[1,2,80,640]{3,2,1,0:T(8,128)S(1)}, f32[16,512]{1,0:T(8,128)S(1)}, f32[2,16,512]{2,1,0:T(8,128)S(1)}) custom-call(f32[1,80,640]{2,1,0:T(8,128)} %fl.1, f32[1,2,80,640]{3,2,1,0:T(8,128)} %ff.1, f32[1,80,640]{2,1,0:T(8,128)} %fd.1, s32[1,80]{1,0:T(1,128)} %shore.1, s32[1,1]{1,0:T(1,128)S(6)} %copy.14.ext, ...), custom_call_target="tpu_custom_call" | custom-call | tf_op jit(solution)/shard_map/nested/pallas_call | solution.py:658
  16.4 0.9 %store.1 = (f32[1,80,640]{2,1,0:T(8,128)}, f32[1,2,80,640]{3,2,1,0:T(8,128)}, f32[16,512]{1,0:T(8,128)}, f32[2,16,512]{2,1,0:T(8,128)}) custom-call(f32[1,80,640]{2,1,0:T(8,128)S(1)} %get-tuple-element.8.refs_0_, f32[1,2,80,640]{3,2,1,0:T(8,128)S(1)} %get-tuple-element.9.refs_1_, f32[16,512]{1,0:T(8,128)S(1)} %get-tuple-element.10.refs_2_, ...), custom_call_target="tpu_custom_call" | custom-call | tf_op jit(solution)/shard_map/store/pallas_call | solution.py:680

commit v5 on v4

--- a/solution.py
+++ b/solution.py
@@ -386,6 +386,18 @@
         for i in range(2):
             q[i, where, edge] = jnp.where(keep, qr[i, where, :], q[i, where, edge])
 
+    arrive(windows)
+    pw = pwb[...]
+    here = lambda x, i: shift_cols(x, 127 - level_at - 16 * i)
+    west_of = lambda x, i: shift_cols(x, 128 - level_at - 16 * i)
+    we, wux, wuy, wd, wwx, wwy = [here(pw, i) for i in range(6)]
+    wuxw, wdw, wwxw = [west_of(pw, i) for i in (1, 3, 4)]
+    whx = 0.5 * (wd + shift_cols(pw, 126 - level_at - 48))
+    whxw = 0.5 * (wdw + wd)
+    why = 0.5 * (wd + shift_rows(wd, -1))
+
+    n1e, n1x, n1xw, n1y = window_step(we, wux, wuxw, wuy)
+    sea = spread_sea(we, wuxw, n1e, n1xw)
     arrive(halo)
     arrive(limits)
     er[halo_n, :] = be[0, 8:16, edge]
@@ -396,18 +408,6 @@
     coefficients(8)
     coefficients(rows - 8 - CH)
 
-    arrive(windows)
-    pw = pwb[...]
-    here = lambda x, i: shift_cols(x, 127 - level_at - 16 * i)
-    west_of = lambda x, i: shift_cols(x, 128 - level_at - 16 * i)
-    we, wux, wuy, wd, wwx, wwy = [here(pw, i) for i in range(6)]
-    wuxw, wdw, wwxw = [west_of(pw, i) for i in (1, 3, 4)]
-    whx = 0.5 * (wd + shift_cols(pw, 126 - level_at - 48))
-    whxw = 0.5 * (wdw + wd)
-    why = 0.5 * (wd + shift_rows(wd, -1))
-
-    n1e, n1x, n1xw, n1y = window_step(we, wux, wuxw, wuy)
-    sea = spread_sea(we, wuxw, n1e, n1xw)
     for n in range(SUBSTEPS):
         advance(be.at[0], bq.at[0], 8, 32, 0)
         advance(be.at[1], bq.at[1], 8, 32, rows - 40)

time: 17.4 us -> 17.2 us (0.989)
  the two profiles are of different devices: /device:TPU:7 before, /device:TPU:0 now
where the time goes in v5:
time: 17.2 us; the launch traced here: 17 us
  Pallas kernels  15.7 us (91%)
  between operations  1.29 us (8%)
    pallas_call x1, Pallas kernels, on_device(): pl.pallas_call(functools.partial(kernel, T, height, breadth, ph, pc), out...  14.8 us
    pallas_call x1, Pallas kernels, on_device(): pl.pallas_call(store, out_shape=[jax.ShapeDtypeStruct(x.shape, f32) for x...  0.88 us

profile of v5, /device:TPU:0, one launch (start us, length us, event | category | flops | bytes accessed | tf_op | source)
XLA Modules:
  0.0 17.0 jit_solution(10181055647785467257)
XLA Ops:
  1.3 14.8 %nested.1 = (f32[1,80,640]{2,1,0:T(8,128)S(1)}, f32[1,2,80,640]{3,2,1,0:T(8,128)S(1)}, f32[16,512]{1,0:T(8,128)S(1)}, f32[2,16,512]{2,1,0:T(8,128)S(1)}) custom-call(f32[1,80,640]{2,1,0:T(8,128)} %fl.1, f32[1,2,80,640]{3,2,1,0:T(8,128)} %ff.1, f32[1,80,640]{2,1,0:T(8,128)} %fd.1, s32[1,80]{1,0:T(1,128)} %shore.1, s32[1,1]{1,0:T(1,128)S(6)} %copy.14.ext, ...), custom_call_target="tpu_custom_call" | custom-call | tf_op jit(solution)/shard_map/nested/pallas_call | solution.py:658
  16.1 0.9 %store.1 = (f32[1,80,640]{2,1,0:T(8,128)}, f32[1,2,80,640]{3,2,1,0:T(8,128)}, f32[16,512]{1,0:T(8,128)}, f32[2,16,512]{2,1,0:T(8,128)}) custom-call(f32[1,80,640]{2,1,0:T(8,128)S(1)} %get-tuple-element.8.refs_0_, f32[1,2,80,640]{3,2,1,0:T(8,128)S(1)} %get-tuple-element.9.refs_1_, f32[16,512]{1,0:T(8,128)S(1)} %get-tuple-element.10.refs_2_, ...), custom_call_target="tpu_custom_call" | custom-call | tf_op jit(solution)/shard_map/store/pallas_call | solution.py:680

commit v6 on v5

--- a/solution.py
+++ b/solution.py
@@ -218,7 +218,7 @@
             Push(fl.at[0, own, :], be.at[b, bs, :], True, d),
             Push(ff.at[0, :, own, :], bq.at[b, :, bs, :], True, d),
         ]
-    start(halo)
+    start([halo[2], halo[5], halo[1], halo[4], halo[0], halo[3]])
 
     pwb[ph:2 * ph, :] = packed_w
 

time: 17.2 us -> 17.2 us (level)
  no operation moved by 1% of the time
where the time goes in v6:
time: 17.2 us; the launch traced here: 17 us
  Pallas kernels  15.7 us (91%)
  between operations  1.29 us (8%)
    pallas_call x1, Pallas kernels, on_device(): pl.pallas_call(functools.partial(kernel, T, height, breadth, ph, pc), out...  14.8 us
    pallas_call x1, Pallas kernels, on_device(): pl.pallas_call(store, out_shape=[jax.ShapeDtypeStruct(x.shape, f32) for x...  0.88 us

profile of v6, /device:TPU:0, one launch (start us, length us, event | category | flops | bytes accessed | tf_op | source)
XLA Modules:
  0.0 17.0 jit_solution(5636607326204414073)
XLA Ops:
  1.3 14.8 %nested.1 = (f32[1,80,640]{2,1,0:T(8,128)S(1)}, f32[1,2,80,640]{3,2,1,0:T(8,128)S(1)}, f32[16,512]{1,0:T(8,128)S(1)}, f32[2,16,512]{2,1,0:T(8,128)S(1)}) custom-call(f32[1,80,640]{2,1,0:T(8,128)} %fl.1, f32[1,2,80,640]{3,2,1,0:T(8,128)} %ff.1, f32[1,80,640]{2,1,0:T(8,128)} %fd.1, s32[1,80]{1,0:T(1,128)} %shore.1, s32[1,1]{1,0:T(1,128)S(6)} %copy.14.ext, ...), custom_call_target="tpu_custom_call" | custom-call | tf_op jit(solution)/shard_map/nested/pallas_call | solution.py:658
  16.1 0.9 %store.1 = (f32[1,80,640]{2,1,0:T(8,128)}, f32[1,2,80,640]{3,2,1,0:T(8,128)}, f32[16,512]{1,0:T(8,128)}, f32[2,16,512]{2,1,0:T(8,128)}) custom-call(f32[1,80,640]{2,1,0:T(8,128)S(1)} %get-tuple-element.8.refs_0_, f32[1,2,80,640]{3,2,1,0:T(8,128)S(1)} %get-tuple-element.9.refs_1_, f32[16,512]{1,0:T(8,128)S(1)} %get-tuple-element.10.refs_2_, ...), custom_call_target="tpu_custom_call" | custom-call | tf_op jit(solution)/shard_map/store/pallas_call | solution.py:680
